TPU v7x, 256 devices: a whole 4x4x8 slice. The times are simulated.
256 devices in a mesh: expert: 32 (over y, z_hi, core), cuts: 8 (over z_lo, x).
Axes of the slice: x: 4, y: 4, z: 8 (z_hi: 4, z_lo: 2; z = z_hi * 2 + z_lo), core: 2. Of those that a mesh axis runs over, the one named last changes fastest.
Arguments:
- tokens: bfloat16 [4096, 3584], P('expert', 'cuts'), may hold values from -6 to 6
- routing: int32 [4096, 8], P('expert'), may hold values from 0 to 31, all different within a row; in each aligned block of 128 rows (0 to 127, 128 to 255, ...) at most 40 rows name the same one
- gate_weights: float32 [4096, 8], P('expert'), may hold values from 0.05 to 0.6
- owner: int32 [32], replicated, may hold values from 0 to 31, each once
- weights: bfloat16 [32, 2, 3584, 1024], P('expert', None, None, 'cuts'), may hold values from -0.09375 to 0.09375
- grads: bfloat16 [32, 2, 3584, 1024], P('expert', None, None, 'cuts'), may hold values from -6 to 6
- first: bfloat16 [32, 2, 3584, 1024], P('expert', None, None, 'cuts'), may hold values from -4 to 4
- second: bfloat16 [32, 2, 3584, 1024], P('expert', None, None, 'cuts'), may hold values from 0.049804688 to 2
Outputs:
- mixed: bfloat16 [4096, 3584], P('expert', 'cuts')
- new_weights: bfloat16 [32, 2, 3584, 1024], P('expert', None, None, 'cuts')
- new_first: bfloat16 [32, 2, 3584, 1024], P('expert', None, None, 'cuts')
- new_second: bfloat16 [32, 2, 3584, 1024], P('expert', None, None, 'cuts')
Inputs may be any that keep to these rules, and one draw needn't show every extreme that they name: `routing`: each row names 8 different experts; among the 128 rows of one device no expert is named more than 40 times, and in every draw some expert is named exactly 40 times there. A permutation: expert e, held at index e of the expert axis before migration, is held at index owner[e] after it.
All inputs are finite; a program needn't handle non-finite values.
Results may differ from a plain program's by a relative error of at most 0.015.
Values may be sent and summed in bfloat16 or wider, within the bound.
No kernel may reach another device: no remote copies, remote signals or barrier semaphores. Data moves between devices by JAX's collectives and lax.ppermute only.
A program may use at most 128 MiB of HBM per device.

v0:
```python
import jax
import jax.numpy as jnp
from jax import lax
from jax.sharding import PartitionSpec as P

beta_first = 0.9
beta_second = 0.95
learning_rate = 0.003
weight_decay = 0.1
epsilon = 1e-08


def adamw_step(weights, grads, first, second):
    gradient = grads.astype(jnp.float32)
    first_new = beta_first * first.astype(jnp.float32) + (1.0 - beta_first) * gradient
    second_new = (
        beta_second * second.astype(jnp.float32) + (1.0 - beta_second) * gradient * gradient
    )
    current = weights.astype(jnp.float32)
    updated = current - learning_rate * (
        first_new / (jnp.sqrt(second_new) + epsilon) + weight_decay * current
    )
    return (
        updated.astype(jnp.bfloat16),
        first_new.astype(jnp.bfloat16),
        second_new.astype(jnp.bfloat16),
    )


def assign_slots(routing, expert_count, capacity):
    chosen = routing.reshape(-1)
    onehot = (chosen[:, None] == jnp.arange(expert_count, dtype=jnp.int32)[None, :]).astype(
        jnp.int32
    )
    earlier = jnp.cumsum(onehot, axis=0) - onehot
    slot_index = jnp.sum(earlier * onehot, axis=1)
    return (chosen * capacity + slot_index).reshape(routing.shape)


def local(tokens, routing, gate_weights, owner, weights, grads, first, second):
    expert_count = owner.shape[0]
    token_count = tokens.shape[0]
    top_count = routing.shape[1]
    capacity = 5 * token_count * top_count // (4 * expert_count)
    updated, first_new, second_new = adamw_step(weights, grads, first, second)
    state_shape = updated.shape
    device_order = jnp.arange(expert_count, dtype=jnp.int32)
    holder = jnp.sum(device_order[None, :] * (owner[None, :] == device_order[:, None]), axis=1)
    spread_w, spread_m, spread_v = (
        lax.all_to_all(
            updated.reshape(expert_count, -1), "expert", split_axis=0, concat_axis=0, tiled=True
        ),
        lax.all_to_all(
            first_new.reshape(expert_count, -1), "expert", split_axis=0, concat_axis=0, tiled=True
        ),
        lax.all_to_all(
            second_new.reshape(expert_count, -1), "expert", split_axis=0, concat_axis=0, tiled=True
        ),
    )
    arrived_w, arrived_m, arrived_v = (
        lax.all_to_all(
            jnp.take(spread_w, holder, axis=0), "expert", split_axis=0, concat_axis=0, tiled=True
        ),
        lax.all_to_all(
            jnp.take(spread_m, holder, axis=0), "expert", split_axis=0, concat_axis=0, tiled=True
        ),
        lax.all_to_all(
            jnp.take(spread_v, holder, axis=0), "expert", split_axis=0, concat_axis=0, tiled=True
        ),
    )
    new_weights = arrived_w.reshape(state_shape)
    new_first = arrived_m.reshape(state_shape)
    new_second = arrived_v.reshape(state_shape)
    position = assign_slots(routing, expert_count, capacity)
    source_token = (
        jnp.full((expert_count * capacity,), token_count, jnp.int32)
        .at[position.reshape(-1)]
        .set(jnp.arange(token_count * top_count, dtype=jnp.int32) // top_count)
    )
    padded = jnp.concatenate([tokens, jnp.zeros((1, tokens.shape[1]), tokens.dtype)], axis=0)
    buffered = jnp.take(padded, source_token, axis=0).reshape(expert_count, capacity, -1)
    serving = new_weights[0]
    outgoing = jnp.take(buffered, holder, axis=0)
    w_up = serving[0]
    w_down = serving[1]
    incoming = lax.all_to_all(outgoing, "expert", split_axis=0, concat_axis=0, tiled=True)
    flat_rows = incoming.reshape(-1, incoming.shape[2])
    pre_active = jnp.dot(
        lax.all_gather(flat_rows, "cuts", axis=1, tiled=True),
        w_up,
        preferred_element_type=jnp.float32,
    )
    hidden = jax.nn.silu(pre_active).astype(jnp.bfloat16)
    down_block = lax.all_to_all(w_down, "cuts", split_axis=0, concat_axis=1, tiled=True)
    group_width = w_down.shape[1]
    piece = lax.all_gather(hidden, "cuts", axis=1, tiled=True)
    group_count = piece.shape[1] // group_width
    products = jnp.einsum(
        "rgf,dgf->grd",
        piece.reshape(piece.shape[0], group_count, group_width),
        down_block.reshape(down_block.shape[0], group_count, group_width),
        preferred_element_type=jnp.float32,
    )
    rounded = lax.optimization_barrier(products.astype(jnp.bfloat16))
    summed = jnp.sum(rounded.astype(jnp.float32), axis=0)
    expert_out = summed.astype(jnp.bfloat16).reshape(expert_count, capacity, -1)
    returned_rows = lax.all_to_all(expert_out, "expert", split_axis=0, concat_axis=0, tiled=True)
    returned_rows = jnp.take(returned_rows, owner, axis=0)
    picked = jnp.take(
        returned_rows.reshape(expert_count * capacity, -1), position.reshape(-1), axis=0
    ).reshape(token_count, top_count, -1)
    mixed = jnp.einsum(
        "tk,tkd->td", gate_weights, picked.astype(jnp.float32), precision=lax.Precision.HIGHEST
    )
    return (mixed.astype(jnp.bfloat16), new_weights, new_first, new_second)


def solution(mesh):
    return jax.shard_map(
        local,
        mesh=mesh,
        in_specs=(
            P("expert", "cuts"),
            P("expert", None),
            P("expert", None),
            P(),
            P("expert", None, None, "cuts"),
            P("expert", None, None, "cuts"),
            P("expert", None, None, "cuts"),
            P("expert", None, None, "cuts"),
        ),
        out_specs=(
            P("expert", "cuts"),
            P("expert", None, None, "cuts"),
            P("expert", None, None, "cuts"),
            P("expert", None, None, "cuts"),
        ),
        check_vma=False,
    )
```

profile of v0, /device:TPU:11, one launch (start us, length us, event | category | flops | bytes accessed | tf_op | source)
XLA Modules:
  0.0 596.4 jit_solution(16376416813683779509)
XLA Ops:
  9.6 9.0 %reduce-window.6 = s32[32,8,128]{2,1,0:T(8,128)S(1)} reduce-window(s32[32,8,128]{2,1,0:T(8,128)S(1)} %fusion.13, s32[]{:T(128)} %constant.59.clone.1), window={size=1x1x128 pad=0_0x0_0x127_0}, to_apply=%region_0.0 | reduce-window | flops 4161536 | bytes 262148 | tf_op jit(solution)/shard_map/reduce-window
  31.1 12.0 %all-to-all-start = ((bf16[32,40,448]{2,1,0:T(8,128)(2,1)}), bf16[32,40,448]{2,1,0:T(8,128)(2,1)S(1)}, u32[]{:S(2)}, u32[]{:S(2)}) async-start(bf16[32,40,448]{2,1,0:T(8,128)(2,1)} %broadcast_select_fusion.1), calls=%async_computation | async-start | bytes 2621440 | tf_op jit(solution)/shard_map/all_to_all | solution.py:86
  53.9 12.4 %reduce.11 = bf16[32,28672]{1,0:T(8,128)(2,1)S(1)} reduce(bf16[32,1,28672]{2,1,0:T(2,128)(2,1)} %all_to_all.81, bf16[]{:T(256)} %broadcast.123), dimensions={1}, to_apply=%all_to_all.81.reduce_sub_computation | reduce | bytes 3670018 | tf_op jit(solution)/shard_map/all_to_all | solution.py:53
  68.6 7.3 %all-to-all-done = bf16[32,40,448]{2,1,0:T(8,128)(2,1)S(1)} async-done(((bf16[32,40,448]{2,1,0:T(8,128)(2,1)}), bf16[32,40,448]{2,1,0:T(8,128)(2,1)S(1)}, u32[]{:S(2)}, u32[]{:S(2)}) %all-to-all-start) | async-done | bytes 1146912 | tf_op jit(solution)/shard_map/all_to_all | solution.py:86
  75.9 7.9 %all-to-all-start.5 = ((bf16[32,2,14336]{2,1,0:T(2,128)(2,1)}), bf16[32,2,14336]{2,1,0:T(2,128)(2,1)}, u32[]{:S(2)}, u32[]{:S(2)}) async-start(bf16[32,2,14336]{2,1,0:T(2,128)(2,1)} %reshape.251), calls=%async_computation.5 | async-start | bytes 3670016 | tf_op jit(solution)/shard_map/all_to_all | solution.py:53
  87.4 12.4 %reduce.10 = bf16[32,28672]{1,0:T(8,128)(2,1)S(1)} reduce(bf16[32,1,28672]{2,1,0:T(2,128)(2,1)} %all_to_all.82, bf16[]{:T(256)} %broadcast.123), dimensions={1}, to_apply=%all_to_all.82.reduce_sub_computation | reduce | bytes 3670018 | tf_op jit(solution)/shard_map/all_to_all | solution.py:56
  102.1 25.5 %all-to-all-done.5 = bf16[32,2,14336]{2,1,0:T(2,128)(2,1)} async-done(((bf16[32,2,14336]{2,1,0:T(2,128)(2,1)}), bf16[32,2,14336]{2,1,0:T(2,128)(2,1)}, u32[]{:S(2)}, u32[]{:S(2)}) %all-to-all-start.5) | async-done | bytes 1835040 | tf_op jit(solution)/shard_map/all_to_all | solution.py:53
  127.7 7.6 %all-to-all-start.7 = ((bf16[32,2,14336]{2,1,0:T(2,128)(2,1)}), bf16[32,2,14336]{2,1,0:T(2,128)(2,1)}, u32[]{:S(2)}, u32[]{:S(2)}) async-start(bf16[32,2,14336]{2,1,0:T(2,128)(2,1)} %reshape.255), calls=%async_computation.7 | async-start | bytes 3670016 | tf_op jit(solution)/shard_map/all_to_all | solution.py:56
  138.9 12.4 %reduce.12 = bf16[32,28672]{1,0:T(8,128)(2,1)S(1)} reduce(bf16[32,1,28672]{2,1,0:T(2,128)(2,1)} %all_to_all.80, bf16[]{:T(256)} %broadcast.123), dimensions={1}, to_apply=%all_to_all.80.reduce_sub_computation | reduce | bytes 3670018 | tf_op jit(solution)/shard_map/all_to_all | solution.py:50
  153.6 25.7 %all-to-all-done.7 = bf16[32,2,14336]{2,1,0:T(2,128)(2,1)} async-done(((bf16[32,2,14336]{2,1,0:T(2,128)(2,1)}), bf16[32,2,14336]{2,1,0:T(2,128)(2,1)}, u32[]{:S(2)}, u32[]{:S(2)}) %all-to-all-start.7) | async-done | bytes 1835040 | tf_op jit(solution)/shard_map/all_to_all | solution.py:56
  179.3 7.2 %all-to-all-start.1 = ((bf16[32,2,14336]{2,1,0:T(2,128)(2,1)}), bf16[32,2,14336]{2,1,0:T(2,128)(2,1)}, u32[]{:S(2)}, u32[]{:S(2)}) async-start(bf16[32,2,14336]{2,1,0:T(2,128)(2,1)} %reshape.247), calls=%async_computation.1 | async-start | bytes 3670016 | tf_op jit(solution)/shard_map/all_to_all | solution.py:50
  188.1 10.2 %reshape.252 = bf16[32,1,28672]{2,1,0:T(2,128)(2,1)} reshape(bf16[32,2,14336]{2,1,0:T(2,128)(2,1)} %all-to-all-done.5) | data formatting | bytes 3670016
  205.4 10.2 %reshape.256 = bf16[32,1,28672]{2,1,0:T(2,128)(2,1)} reshape(bf16[32,2,14336]{2,1,0:T(2,128)(2,1)} %all-to-all-done.7) | data formatting | bytes 3670016
  222.7 7.7 %all-to-all-done.1 = bf16[32,2,14336]{2,1,0:T(2,128)(2,1)} async-done(((bf16[32,2,14336]{2,1,0:T(2,128)(2,1)}), bf16[32,2,14336]{2,1,0:T(2,128)(2,1)}, u32[]{:S(2)}, u32[]{:S(2)}) %all-to-all-start.1) | async-done | bytes 1835040 | tf_op jit(solution)/shard_map/all_to_all | solution.py:50
  230.4 10.2 %reshape.248 = bf16[32,1,28672]{2,1,0:T(2,128)(2,1)} reshape(bf16[32,2,14336]{2,1,0:T(2,128)(2,1)} %all-to-all-done.1) | data formatting | bytes 3670016
  256.6 11.5 %reshape.249 = bf16[32,2,14336]{2,1,0:T(2,128)(2,1)} reshape(bf16[32,28672]{1,0:T(8,128)(2,1)S(1)} %reduce.13) | data formatting | bytes 3670016
  268.0 7.3 %all-to-all-start.2 = ((bf16[32,2,14336]{2,1,0:T(2,128)(2,1)}), bf16[32,2,14336]{2,1,0:T(2,128)(2,1)}, u32[]{:S(2)}, u32[]{:S(2)}) async-start(bf16[32,2,14336]{2,1,0:T(2,128)(2,1)} %reshape.249), calls=%async_computation.2 | async-start | bytes 3670016 | tf_op jit(solution)/shard_map/all_to_all | solution.py:61
  281.2 38.4 %all-to-all-done.2 = bf16[32,2,14336]{2,1,0:T(2,128)(2,1)} async-done(((bf16[32,2,14336]{2,1,0:T(2,128)(2,1)}), bf16[32,2,14336]{2,1,0:T(2,128)(2,1)}, u32[]{:S(2)}, u32[]{:S(2)}) %all-to-all-start.2) | async-done | bytes 1835040 | tf_op jit(solution)/shard_map/all_to_all | solution.py:61
  326.7 10.2 %reshape.250 = bf16[32,1,28672]{2,1,0:T(2,128)(2,1)} reshape(bf16[32,2,14336]{2,1,0:T(2,128)(2,1)} %all-to-all-done.2) | data formatting | bytes 3670016
  336.9 10.7 %slice_reduce_fusion = (bf16[16,28672]{1,0:T(8,128)(2,1)S(1)}, bf16[16,28672]{1,0:T(8,128)(2,1)}) fusion(bf16[32,1,28672]{2,1,0:T(2,128)(2,1)} %reshape.250), kind=kLoop, calls=%fused_computation.23 | loop fusion | bytes 3670016 | tf_op jit(solution)/shard_map/slice | solution.py:85
  351.6 19.3 %all-to-all-done.6 = bf16[32,2,14336]{2,1,0:T(2,128)(2,1)S(1)} async-done(((bf16[32,2,14336]{2,1,0:T(2,128)(2,1)}), bf16[32,2,14336]{2,1,0:T(2,128)(2,1)S(1)}, u32[]{:S(2)}, u32[]{:S(2)}) %all-to-all-start.6) | async-done | bytes 1835040 | tf_op jit(solution)/shard_map/all_to_all | solution.py:64
  371.0 35.1 %all-to-all-start.3 = ((bf16[8,448,128]{2,1,0:T(8,128)(2,1)}), bf16[8,448,128]{2,1,0:T(8,128)(2,1)S(1)}, u32[]{:S(2)}, u32[]{:S(2)}) async-start(bf16[8,448,128]{2,1,0:T(8,128)(2,1)} %all_to_all.66), calls=%async_computation.3 | async-start | bytes 1835008 | tf_op jit(solution)/shard_map/all_to_all | solution.py:94
  406.3 7.1 %multiply_convert_fusion = bf16[1280,128]{1,0:T(8,128)(2,1)} fusion(bf16[1280,3584]{0,1:T(8,128)(2,1)} %all-gather.3.cloned.1.call-done, bf16[3584,128]{1,0:T(8,128)(2,1)} %squeeze.4), kind=kOutput, calls=%fused_computation.36 | convolution fusion | flops 1175224320 | bytes 10420224 | tf_op jit(solution)/shard_map/dot_general | solution.py:88
  419.4 7.3 %all-to-all-start.8 = ((bf16[32,2,14336]{2,1,0:T(2,128)(2,1)}), bf16[32,2,14336]{2,1,0:T(2,128)(2,1)S(1)}, u32[]{:S(2)}, u32[]{:S(2)}) async-start(bf16[32,2,14336]{2,1,0:T(2,128)(2,1)} %reshape.257), calls=%async_computation.8 | async-start | bytes 3670016 | tf_op jit(solution)/shard_map/all_to_all | solution.py:67
  426.7 64.1 %all-gather.5.cloned.1.call-done = bf16[1280,1024]{1,0:T(8,128)(2,1)} async-done(((bf16[1280,128]{1,0:T(8,128)(2,1)}), bf16[1280,1024]{1,0:T(8,128)(2,1)}) %all-gather.5.cloned.1.call-update) | async-done | bytes 2621456 | tf_op jit(solution)/shard_map/all_gather | solution.py:96
  490.8 7.8 %convolution_convert_fusion = bf16[8,1280,448]{1,2,0:T(8,128)(2,1)} fusion(bf16[8,448,128]{2,1,0:T(8,128)(2,1)S(1)} %all-to-all-done.3, bf16[1280,1024]{1,0:T(8,128)(2,1)} %all-gather.5.cloned.1.call-done), kind=kOutput, calls=%fused_computation.8 | convolution fusion | flops 1178992640 | bytes 12713984 | tf_op jit(solution)/shard_map/rgf,dgf->grd/dot_general | solution.py:98
  505.7 13.1 %all-to-all-start.4 = ((bf16[32,40,448]{2,1,0:T(8,128)(2,1)}), bf16[32,40,448]{2,1,0:T(8,128)(2,1)S(1)}, u32[]{:S(2)}, u32[]{:S(2)}) async-start(bf16[32,40,448]{2,1,0:T(8,128)(2,1)} %bitcast.8), calls=%async_computation.4 | async-start | bytes 2621440 | tf_op jit(solution)/shard_map/all_to_all | solution.py:107
  519.2 11.8 %reduce.4 = bf16[32,28672]{1,0:T(8,128)(2,1)S(1)} reduce(bf16[32,1,28672]{2,1,0:T(2,128)(2,1)} %reshape.250, bf16[]{:T(256)} %constant.104), dimensions={1}, to_apply=%all_to_all.65.reduce_sub_computation | reduce | bytes 3670018 | tf_op jit(solution)/shard_map/all_to_all | solution.py:61
  532.8 10.2 %reshape.254 = bf16[32,1,28672]{2,1,0:T(2,128)(2,1)} reshape(bf16[32,2,14336]{2,1,0:T(2,128)(2,1)} %copy-done) | data formatting | bytes 3670016
  543.0 11.8 %reduce.5 = bf16[32,28672]{1,0:T(8,128)(2,1)S(1)} reduce(bf16[32,1,28672]{2,1,0:T(2,128)(2,1)} %reshape.254, bf16[]{:T(256)} %constant.104), dimensions={1}, to_apply=%all_to_all.74.reduce_sub_computation | reduce | bytes 3670018 | tf_op jit(solution)/shard_map/all_to_all | solution.py:64
  556.5 10.2 %reshape.258 = bf16[32,1,28672]{2,1,0:T(2,128)(2,1)} reshape(bf16[32,2,14336]{2,1,0:T(2,128)(2,1)} %copy-done.1) | data formatting | bytes 3670016
  566.8 11.8 %reduce.6 = bf16[32,28672]{1,0:T(8,128)(2,1)S(1)} reduce(bf16[32,1,28672]{2,1,0:T(2,128)(2,1)} %reshape.258, bf16[]{:T(256)} %constant.104), dimensions={1}, to_apply=%all_to_all.79.reduce_sub_computation | reduce | bytes 3670018 | tf_op jit(solution)/shard_map/all_to_all | solution.py:67
  (96 shorter events, 115.7 us)
Async XLA Ops:
  31.1 44.8 %all-to-all-start = ((bf16[32,40,448]{2,1,0:T(8,128)(2,1)}), bf16[32,40,448]{2,1,0:T(8,128)(2,1)S(1)}, u32[]{:S(2)}, u32[]{:S(2)}) async-start(bf16[32,40,448]{2,1,0:T(8,128)(2,1)} %broadcast_select_fusion.1), calls=%async_computation | async-start | bytes 2621440 | tf_op jit(solution)/shard_map/all_to_all | solution.py:86
  68.6 15.2 %copy-start.3 = (bf16[1,2,3584,128]{3,2,1,0:T(8,128)(2,1)S(1)}, bf16[1,2,3584,128]{3,2,1,0:T(8,128)(2,1)}, u32[]{:S(2)}) copy-start(bf16[1,2,3584,128]{3,2,1,0:T(8,128)(2,1)} %get-tuple-element.8) | copy-start | bytes 5505028
  75.9 51.8 %all-to-all-start.5 = ((bf16[32,2,14336]{2,1,0:T(2,128)(2,1)}), bf16[32,2,14336]{2,1,0:T(2,128)(2,1)}, u32[]{:S(2)}, u32[]{:S(2)}) async-start(bf16[32,2,14336]{2,1,0:T(2,128)(2,1)} %reshape.251), calls=%async_computation.5 | async-start | bytes 3670016 | tf_op jit(solution)/shard_map/all_to_all | solution.py:53
  102.1 33.1 %copy-start.2 = (bf16[1,2,3584,128]{3,2,1,0:T(8,128)(2,1)S(1)}, bf16[1,2,3584,128]{3,2,1,0:T(8,128)(2,1)}, u32[]{:S(2)}) copy-start(bf16[1,2,3584,128]{3,2,1,0:T(8,128)(2,1)} %get-tuple-element.9) | copy-start | bytes 5505028
  127.7 51.6 %all-to-all-start.7 = ((bf16[32,2,14336]{2,1,0:T(2,128)(2,1)}), bf16[32,2,14336]{2,1,0:T(2,128)(2,1)}, u32[]{:S(2)}, u32[]{:S(2)}) async-start(bf16[32,2,14336]{2,1,0:T(2,128)(2,1)} %reshape.255), calls=%async_computation.7 | async-start | bytes 3670016 | tf_op jit(solution)/shard_map/all_to_all | solution.py:56
  179.3 51.1 %all-to-all-start.1 = ((bf16[32,2,14336]{2,1,0:T(2,128)(2,1)}), bf16[32,2,14336]{2,1,0:T(2,128)(2,1)}, u32[]{:S(2)}, u32[]{:S(2)}) async-start(bf16[32,2,14336]{2,1,0:T(2,128)(2,1)} %reshape.247), calls=%async_computation.1 | async-start | bytes 3670016 | tf_op jit(solution)/shard_map/all_to_all | solution.py:50
  186.5 219.8 %all-gather.3.cloned.1.call-start = ((), (), s32[]{:S(2)}) async-start(), calls=%async_computation.9 | async-start | bytes 10321920 | tf_op jit(solution)/shard_map/all_gather | solution.py:89
  268.0 51.6 %all-to-all-start.2 = ((bf16[32,2,14336]{2,1,0:T(2,128)(2,1)}), bf16[32,2,14336]{2,1,0:T(2,128)(2,1)}, u32[]{:S(2)}, u32[]{:S(2)}) async-start(bf16[32,2,14336]{2,1,0:T(2,128)(2,1)} %reshape.249), calls=%async_computation.2 | async-start | bytes 3670016 | tf_op jit(solution)/shard_map/all_to_all | solution.py:61
  319.6 51.3 %all-to-all-start.6 = ((bf16[32,2,14336]{2,1,0:T(2,128)(2,1)}), bf16[32,2,14336]{2,1,0:T(2,128)(2,1)S(1)}, u32[]{:S(2)}, u32[]{:S(2)}) async-start(bf16[32,2,14336]{2,1,0:T(2,128)(2,1)} %reshape.253), calls=%async_computation.6 | async-start | bytes 3670016 | tf_op jit(solution)/shard_map/all_to_all | solution.py:64
  371.0 42.5 %copy-start = (bf16[32,2,14336]{2,1,0:T(2,128)(2,1)}, bf16[32,2,14336]{2,1,0:T(2,128)(2,1)S(1)}, u32[]{:S(2)}) copy-start(bf16[32,2,14336]{2,1,0:T(2,128)(2,1)S(1)} %all-to-all-done.6) | copy-start | bytes 5505028
  371.0 48.4 %all-to-all-start.3 = ((bf16[8,448,128]{2,1,0:T(8,128)(2,1)}), bf16[8,448,128]{2,1,0:T(8,128)(2,1)S(1)}, u32[]{:S(2)}, u32[]{:S(2)}) async-start(bf16[8,448,128]{2,1,0:T(8,128)(2,1)} %all_to_all.66), calls=%async_computation.3 | async-start | bytes 1835008 | tf_op jit(solution)/shard_map/all_to_all | solution.py:94
  406.1 84.7 %all-gather.5.cloned.1.call-start = ((), (), s32[]{:S(2)}) async-start(), calls=%async_computation.10 | async-start | bytes 2949120 | tf_op jit(solution)/shard_map/all_gather | solution.py:96
  419.4 86.3 %all-to-all-start.8 = ((bf16[32,2,14336]{2,1,0:T(2,128)(2,1)}), bf16[32,2,14336]{2,1,0:T(2,128)(2,1)S(1)}, u32[]{:S(2)}, u32[]{:S(2)}) async-start(bf16[32,2,14336]{2,1,0:T(2,128)(2,1)} %reshape.257), calls=%async_computation.8 | async-start | bytes 3670016 | tf_op jit(solution)/shard_map/all_to_all | solution.py:67
  505.6 13.2 %copy-start.4 = (s32[128,8]{0,1:T(8,128)S(1)}, s32[128,8]{0,1:T(8,128)}, u32[]{:S(2)}) copy-start(s32[128,8]{0,1:T(8,128)} %param.13) | copy-start | bytes 12292
  505.6 13.4 %copy-start.5 = (f32[128,8]{0,1:T(8,128)S(1)}, f32[128,8]{0,1:T(8,128)}, u32[]{:S(2)}) copy-start(f32[128,8]{0,1:T(8,128)} %param.14) | copy-start | bytes 12292
  505.7 13.5 %copy-start.6 = (s32[32]{0:T(128)S(1)}, s32[32]{0:T(128)}, u32[]{:S(2)}) copy-start(s32[32]{0:T(128)} %param.15) | copy-start | bytes 388
  505.7 13.5 %copy-start.1 = (bf16[32,2,14336]{2,1,0:T(2,128)(2,1)}, bf16[32,2,14336]{2,1,0:T(2,128)(2,1)S(1)}, u32[]{:S(2)}) copy-start(bf16[32,2,14336]{2,1,0:T(2,128)(2,1)S(1)} %all-to-all-done.8) | copy-start | bytes 5505028
  505.7 74.7 %all-to-all-start.4 = ((bf16[32,40,448]{2,1,0:T(8,128)(2,1)}), bf16[32,40,448]{2,1,0:T(8,128)(2,1)S(1)}, u32[]{:S(2)}, u32[]{:S(2)}) async-start(bf16[32,40,448]{2,1,0:T(8,128)(2,1)} %bitcast.8), calls=%async_computation.4 | async-start | bytes 2621440 | tf_op jit(solution)/shard_map/all_to_all | solution.py:107
Sparse Core Ops, SparseCore 0:
  189.2 146.8 all-gather.2
  413.6 77.1 all-gather.4
where the time goes:
time: 608 us; the launch traced here: 596 us
  waiting for transfers between devices  188 us (31%)
  local copies, waits for them, and re-layouts  158 us (26%)
  other arithmetic  115 us (19%)
  starting transfers between devices  105 us (17%)
  matrix products  15 us (2%)
  between operations  14.9 us (2%)
    unnamed x32, local copies, waits for them, and re-layouts  98.5 us
    all_gather x1, waiting for transfers between devices, local(): piece = lax.all_gather(hidden, 'cuts', axis=1, tiled=True)  64.1 us
    all_to_all x1, waiting for transfers between devices, local(): lax.all_to_all(jnp.take(spread_w, holder, axis=0), 'expert', split_axis=0...  38.4 us
    all_to_all x1, starting transfers between devices, local(): lax.all_to_all(w_down, 'cuts', split_axis=0, concat_axis=1, tiled=True)  35.1 us
    all_to_all x1, waiting for transfers between devices, local(): lax.all_to_all(second_new.reshape(expert_count, -1), 'expert', split_axis...  25.7 us
    all_to_all x1, waiting for transfers between devices, local(): lax.all_to_all(first_new.reshape(expert_count, -1), 'expert', split_axis=...  25.5 us
    all_to_all x3, other arithmetic, local(): lax.all_to_all(jnp.take(spread_v, holder, axis=0), 'expert', split_axis=0...  20.6 us
    all_to_all x1, waiting for transfers between devices, local(): lax.all_to_all(jnp.take(spread_m, holder, axis=0), 'expert', split_axis=0...  19.3 us
  transfers between devices with their start and end apart: 11, of which 7 were waited for; matrix products, arithmetic and copies ran while one was open for 41% of the time, Pallas kernels for 0%

commit v1 on v0

v1 whole, which is shorter than its diff:
```python
import jax
import jax.numpy as jnp
from jax import lax
from jax.experimental import pallas as pl
from jax.experimental.pallas import tpu as pltpu
from jax.sharding import PartitionSpec as P

beta_first = 0.9
beta_second = 0.95
learning_rate = 0.003
weight_decay = 0.1
epsilon = 1e-08


def adamw_kernel(weights, grads, first, second, updated_out, first_out, second_out):
    gradient = grads[...].astype(jnp.float32)
    first_new = beta_first * first[...].astype(jnp.float32) + (1.0 - beta_first) * gradient
    second_new = (
        beta_second * second[...].astype(jnp.float32)
        + (1.0 - beta_second) * gradient * gradient
    )
    current = weights[...].astype(jnp.float32)
    updated = current - learning_rate * (
        first_new / (jnp.sqrt(second_new) + epsilon) + weight_decay * current
    )
    updated_out[...] = updated.astype(jnp.bfloat16)
    first_out[...] = first_new.astype(jnp.bfloat16)
    second_out[...] = second_new.astype(jnp.bfloat16)


def adamw(weights, grads, first, second, steps):
    rows, lanes = weights.shape
    block = pl.BlockSpec((rows // steps, lanes), lambda i: (i, 0))
    shape = jax.ShapeDtypeStruct((rows, lanes), jnp.bfloat16)
    return pl.pallas_call(
        adamw_kernel,
        grid=(steps,),
        in_specs=[block] * 4,
        out_specs=[block] * 3,
        out_shape=[shape] * 3,
        cost_estimate=pl.CostEstimate(
            flops=12 * rows * lanes, bytes_accessed=14 * rows * lanes, transcendentals=rows * lanes
        ),
        name="adamw",
    )(weights, grads, first, second)


def up_kernel(rows, weights, out):
    for group in range(weights.shape[0]):
        out[group] = jnp.dot(
            rows[...], weights[group], preferred_element_type=jnp.float32
        ).astype(jnp.bfloat16)


def up_project(rows, weights, steps):
    count, features = rows.shape
    groups, _, width = weights.shape
    return pl.pallas_call(
        up_kernel,
        grid=(steps,),
        in_specs=[
            pl.BlockSpec((count // steps, features), lambda i: (i, 0)),
            pl.BlockSpec((groups, features, width), lambda i: (0, 0, 0)),
        ],
        out_specs=pl.BlockSpec((groups, count // steps, width), lambda i: (0, i, 0)),
        out_shape=jax.ShapeDtypeStruct((groups, count, width), jnp.bfloat16),
        cost_estimate=pl.CostEstimate(
            flops=2 * count * features * groups * width,
            bytes_accessed=2 * (count * features + groups * width * (features + count)),
            transcendentals=0,
        ),
        name="up_project",
    )(rows, weights)


def down_kernel(hidden, weights, out):
    total = jnp.zeros(out.shape, jnp.float32)
    for group in range(weights.shape[0]):
        total += lax.dot_general(
            hidden[group],
            weights[group],
            (((1,), (1,)), ((), ())),
            preferred_element_type=jnp.float32,
        ).astype(jnp.bfloat16).astype(jnp.float32)
    out[...] = total.astype(jnp.bfloat16)


def down_project(hidden, weights, steps):
    groups, count, width = hidden.shape
    features = weights.shape[1]
    return pl.pallas_call(
        down_kernel,
        grid=(steps,),
        in_specs=[
            pl.BlockSpec((groups, count // steps, width), lambda i: (0, i, 0)),
            pl.BlockSpec((groups, features, width), lambda i: (0, 0, 0)),
        ],
        out_specs=pl.BlockSpec((count // steps, features), lambda i: (i, 0)),
        out_shape=jax.ShapeDtypeStruct((count, features), jnp.bfloat16),
        cost_estimate=pl.CostEstimate(
            flops=2 * count * features * groups * width,
            bytes_accessed=2 * (count * features + groups * width * (features + count)),
            transcendentals=0,
        ),
        name="down_project",
    )(hidden, weights)


def exchange(array, axis):
    return lax.all_to_all(array, axis, split_axis=0, concat_axis=0, tiled=True)


def local(tokens, routing, gate_weights, owner, weights, grads, first, second):
    expert_count = owner.shape[0]
    cut_count = lax.axis_size("cuts")
    token_count, features = tokens.shape
    top_count = routing.shape[1]
    capacity = 5 * token_count * top_count // (4 * expert_count)
    state_shape = weights.shape
    width = state_shape[3]
    model = state_shape[2]
    order = jnp.arange(expert_count, dtype=jnp.int32)

    flat = [array.reshape(-1, width) for array in (weights, grads, first, second)]
    updated, first_new, second_new = adamw(*flat, 7)

    matches = routing[:, :, None] == order[None, None, :]
    named = jnp.any(matches, axis=1)
    gate = jnp.sum(jnp.where(matches, gate_weights[:, :, None], 0.0), axis=1)
    positions = jnp.arange(token_count, dtype=jnp.int32)
    earlier = (positions[None, :] < positions[:, None]).astype(jnp.bfloat16)
    slot = jnp.dot(
        earlier, named.astype(jnp.bfloat16), preferred_element_type=jnp.float32
    ).astype(jnp.int32)
    slot = jnp.where(named, slot, -1)
    slots = jnp.arange(capacity, dtype=jnp.int32)
    place = slot.T[:, None, :] == slots[None, :, None]
    buffered = jnp.dot(
        place.astype(jnp.bfloat16).reshape(expert_count * capacity, token_count),
        tokens,
        preferred_element_type=jnp.float32,
    ).astype(jnp.bfloat16)
    incoming = exchange(buffered.reshape(expert_count, capacity, features), "expert")

    split = updated.reshape(2, cut_count, features, width)
    up_block = exchange(split[0], "cuts")
    down_block = exchange(split[1], "cuts")
    parts = up_project(incoming.reshape(-1, features), up_block, 5)
    pre_active = lax.psum_scatter(parts, "cuts", scatter_dimension=0, tiled=False)
    hidden = jax.nn.silu(pre_active.astype(jnp.float32)).astype(jnp.bfloat16)
    every = lax.all_gather(hidden, "cuts", axis=0, tiled=False)
    expert_out = down_project(every, down_block, 5)
    returned = exchange(expert_out.reshape(expert_count, capacity, features), "expert")

    share = jnp.where(
        slot[:, :, None] == slots[None, None, :], gate[:, :, None], 0.0
    ).reshape(token_count, expert_count * capacity)
    mixed = jnp.dot(
        share,
        returned.reshape(expert_count * capacity, features).astype(jnp.float32),
        precision=lax.Precision.HIGHEST,
        preferred_element_type=jnp.float32,
    ).astype(jnp.bfloat16)

    holder = jnp.sum(order[None, :] * (owner[None, :] == order[:, None]), axis=1)
    moved = []
    for array in (updated, first_new, second_new):
        spread = exchange(array.reshape(expert_count, -1, width), "expert")
        arrived = exchange(jnp.take(spread, holder, axis=0), "expert")
        moved.append(arrived.reshape(state_shape))
    return (mixed, *moved)


def solution(mesh):
    state = P("expert", None, None, "cuts")
    return jax.shard_map(
        local,
        mesh=mesh,
        in_specs=(
            P("expert", "cuts"),
            P("expert", None),
            P("expert", None),
            P(),
            state,
            state,
            state,
            state,
        ),
        out_specs=(P("expert", "cuts"), state, state, state),
        check_vma=False,
    )
```

time: 608 us -> 492 us (0.81)
  the two profiles are of different devices: /device:TPU:11 before, /device:TPU:1 now
where the time goes in v1:
time: 492 us; the launch traced here: 485 us
  waiting for transfers between devices  243 us (49%)
  blocking collectives  145 us (29%)
  starting transfers between devices  30.5 us (6%)
  Pallas kernels  21.8 us (4%)
  local copies, waits for them, and re-layouts  20.3 us (4%)
  between operations  14.2 us (3%)
  other arithmetic  7.04 us (1%)
    all_to_all x6, waiting for transfers between devices, exchange(): return lax.all_to_all(array, axis, split_axis=0, concat_axis=0, tiled=True)  179 us
    all_to_all x4, blocking collectives, exchange(): return lax.all_to_all(array, axis, split_axis=0, concat_axis=0, tiled=True)  145 us
    all_gather x1, waiting for transfers between devices, local(): every = lax.all_gather(hidden, 'cuts', axis=0, tiled=False)  40 us
    all_to_all x6, starting transfers between devices, exchange(): return lax.all_to_all(array, axis, split_axis=0, concat_axis=0, tiled=True)  30.5 us
    reduce_scatter x1, waiting for transfers between devices, local(): lax.psum_scatter(parts, 'cuts', scatter_dimension=0, tiled=False)  24.6 us
  transfers between devices with their start and end apart: 8, of which 8 were waited for; matrix products, arithmetic and copies ran while one was open for 4% of the time, Pallas kernels for 3%

profile of v1, /device:TPU:1, one launch (start us, length us, event | category | flops | bytes accessed | tf_op | source)
XLA Modules:
  0.0 485.2 jit_solution(4184719263855244060)
XLA Ops:
  7.2 8.8 %adamw.1 = (bf16[7168,128]{1,0:T(8,128)(2,1)}, bf16[7168,128]{1,0:T(8,128)(2,1)}, bf16[7168,128]{1,0:T(8,128)(2,1)}) custom-call(bf16[7168,128]{1,0:T(8,128)(2,1)} %bitcast.32, bf16[7168,128]{1,0:T(8,128)(2,1)} %bitcast.33, bf16[7168,128]{1,0:T(8,128)(2,1)} %bitcast.34, bf16[7168,128]{1,0:T(8,128)(2,1)} %bitcast.35), custom_call_target="tpu_custom_call" | custom-call | flops 11010048 | bytes 12845056 | tf_op jit(solution)/shard_map/adamw/pallas_call | solution.py:35
  16.0 1.6 fusion.12
  17.6 19.1 %all_to_all.50.weights = bf16[8,448,128]{2,1,0:T(8,128)(2,1)} all-to-all(bf16[8,448,128]{2,1,0:T(8,128)(2,1)S(1)} %bitcast.31), channel_id=1, replica_groups=mesh['expert'=32,'cuts'=8] {'cuts'}, dimensions={0} | all-to-all | bytes 1835008 | tf_op jit(solution)/shard_map/all_to_all | solution.py:110
  36.7 14.6 %all_to_all.51.weights = bf16[8,448,128]{2,1,0:T(8,128)(2,1)} all-to-all(bf16[8,448,128]{2,1,0:T(8,128)(2,1)S(1)} %bitcast.30), channel_id=1, replica_groups=mesh['expert'=32,'cuts'=8] {'cuts'}, dimensions={0} | all-to-all | bytes 1835008 | tf_op jit(solution)/shard_map/all_to_all | solution.py:110
  51.3 59.6 %all_to_all.52 = bf16[32,224,128]{2,1,0:T(8,128)(2,1)S(1)} all-to-all(bf16[32,224,128]{2,1,0:T(8,128)(2,1)S(1)} %bitcast.27), channel_id=1, replica_groups=mesh['expert'=32,'cuts'=8] {'expert'}, dimensions={0} | all-to-all | bytes 3670016 | tf_op jit(solution)/shard_map/all_to_all | solution.py:110
  110.9 51.8 %all_to_all.53 = bf16[32,224,128]{2,1,0:T(8,128)(2,1)} all-to-all(bf16[32,224,128]{2,1,0:T(8,128)(2,1)S(1)} %bitcast.37), channel_id=1, replica_groups=mesh['expert'=32,'cuts'=8] {'expert'}, dimensions={0} | all-to-all | bytes 3670016 | tf_op jit(solution)/shard_map/all_to_all | solution.py:110
  162.7 5.3 %all-to-all-start.8 = ((bf16[32,224,128]{2,1,0:T(8,128)(2,1)}), bf16[32,224,128]{2,1,0:T(8,128)(2,1)}, u32[]{:S(2)}, u32[]{:S(2)}) async-start(bf16[32,224,128]{2,1,0:T(8,128)(2,1)} %bitcast.36), calls=%async_computation.9 | async-start | bytes 3670016 | tf_op jit(solution)/shard_map/all_to_all | solution.py:110
  169.0 1.5 copy.21
  170.5 43.7 %all-to-all-done.8 = bf16[32,224,128]{2,1,0:T(8,128)(2,1)} async-done(((bf16[32,224,128]{2,1,0:T(8,128)(2,1)}), bf16[32,224,128]{2,1,0:T(8,128)(2,1)}, u32[]{:S(2)}, u32[]{:S(2)}) %all-to-all-start.8) | async-done | bytes 1835040 | tf_op jit(solution)/shard_map/all_to_all | solution.py:110
  214.2 4.6 all-to-all-start
  219.0 2.0 gather_fusion
  221.0 3.5 gather_fusion.1
  224.5 3.6 gather_fusion.2
  228.1 4.7 broadcast_select_fusion
  232.8 19.9 %all-to-all-done = bf16[32,40,448]{2,1,0:T(8,128)(2,1)S(1)} async-done(((bf16[32,40,448]{2,1,0:T(8,128)(2,1)}), bf16[32,40,448]{2,1,0:T(8,128)(2,1)S(1)}, u32[]{:S(2)}, u32[]{:S(2)}) %all-to-all-start) | async-done | bytes 1146912 | tf_op jit(solution)/shard_map/all_to_all | solution.py:110
  253.8 6.3 %all-to-all-start.5 = ((bf16[32,224,128]{2,1,0:T(8,128)(2,1)}), bf16[32,224,128]{2,1,0:T(8,128)(2,1)S(1)}, u32[]{:S(2)}, u32[]{:S(2)}) async-start(bf16[32,224,128]{2,1,0:T(8,128)(2,1)} %get-tuple-element.15), calls=%async_computation.6 | async-start | bytes 3670016 | tf_op jit(solution)/shard_map/all_to_all | solution.py:110
  260.1 6.5 %up_project.1 = bf16[8,1280,128]{2,1,0:T(8,128)(2,1)} custom-call(bf16[1280,448]{1,0:T(8,128)(2,1)} %bitcast.28, bf16[8,448,128]{2,1,0:T(8,128)(2,1)} %all_to_all.50.weights), custom_call_target="tpu_custom_call" | custom-call | flops 1174405120 | bytes 4685824 | tf_op jit(solution)/shard_map/up_project/pallas_call | solution.py:58
  266.7 50.1 %all-to-all-done.5 = bf16[32,224,128]{2,1,0:T(8,128)(2,1)S(1)} async-done(((bf16[32,224,128]{2,1,0:T(8,128)(2,1)}), bf16[32,224,128]{2,1,0:T(8,128)(2,1)S(1)}, u32[]{:S(2)}, u32[]{:S(2)}) %all-to-all-start.5) | async-done | bytes 1835040 | tf_op jit(solution)/shard_map/all_to_all | solution.py:110
  316.8 5.1 %all-to-all-start.7 = ((bf16[32,224,128]{2,1,0:T(8,128)(2,1)}), bf16[32,224,128]{2,1,0:T(8,128)(2,1)}, u32[]{:S(2)}, u32[]{:S(2)}) async-start(bf16[32,224,128]{2,1,0:T(8,128)(2,1)} %get-tuple-element.14), calls=%async_computation.8 | async-start | bytes 3670016 | tf_op jit(solution)/shard_map/all_to_all | solution.py:110
  322.0 24.6 %reduce-scatter.2.cloned.1.call-done = bf16[1,1280,128]{2,1,0:T(8,128)(2,1)} async-done(((bf16[8,1280,128]{2,1,0:T(8,128)(2,1)}), bf16[1,1280,128]{2,1,0:T(8,128)(2,1)}) %reduce-scatter.2.cloned.1.call-update) | async-done | bytes 327696 | tf_op jit(solution)/shard_map/reduce_scatter | solution.py:149
  346.6 1.9 fusion.5
  348.5 26.6 %all-to-all-done.7 = bf16[32,224,128]{2,1,0:T(8,128)(2,1)} async-done(((bf16[32,224,128]{2,1,0:T(8,128)(2,1)}), bf16[32,224,128]{2,1,0:T(8,128)(2,1)}, u32[]{:S(2)}, u32[]{:S(2)}) %all-to-all-start.7) | async-done | bytes 1835040 | tf_op jit(solution)/shard_map/all_to_all | solution.py:110
  375.2 4.8 all-to-all-start.9
  379.9 40.0 %all-gather.2.cloned.1.call-done.hidden = bf16[8,1280,128]{2,1,0:T(8,128)(2,1)} async-done(((bf16[1,1280,128]{2,1,0:T(8,128)(2,1)}), bf16[8,1280,128]{2,1,0:T(8,128)(2,1)}) %all-gather.2.cloned.1.call-update) | async-done | bytes 2621456 | tf_op jit(solution)/shard_map/all_gather | solution.py:151
  419.9 6.5 %down_project.1 = bf16[1280,448]{1,0:T(8,128)(2,1)} custom-call(bf16[8,1280,128]{2,1,0:T(8,128)(2,1)} %all-gather.2.cloned.1.call-done.hidden, bf16[8,448,128]{2,1,0:T(8,128)(2,1)} %all_to_all.51.weights), custom_call_target="tpu_custom_call" | custom-call | flops 1174405120 | bytes 4685824 | tf_op jit(solution)/shard_map/down_project/pallas_call | solution.py:91
  426.4 10.0 %all-to-all-done.9 = bf16[32,224,128]{2,1,0:T(8,128)(2,1)} async-done(((bf16[32,224,128]{2,1,0:T(8,128)(2,1)}), bf16[32,224,128]{2,1,0:T(8,128)(2,1)}, u32[]{:S(2)}, u32[]{:S(2)}) %all-to-all-start.9) | async-done | bytes 1835040 | tf_op jit(solution)/shard_map/all_to_all | solution.py:110
  436.4 4.4 all-to-all-start.3
  440.9 28.4 %all-to-all-done.3 = bf16[32,40,448]{2,1,0:T(8,128)(2,1)S(1)} async-done(((bf16[32,40,448]{2,1,0:T(8,128)(2,1)}), bf16[32,40,448]{2,1,0:T(8,128)(2,1)S(1)}, u32[]{:S(2)}, u32[]{:S(2)}) %all-to-all-start.3) | async-done | bytes 1146912 | tf_op jit(solution)/shard_map/all_to_all | solution.py:110
  469.2 2.2 fusion
  471.4 1.2 copy.27
  472.7 2.8 copy.28
  475.5 2.8 copy.29
  (31 shorter events, 2.3 us)
Async XLA Ops:
  7.2 161.4 %copy-start = (bf16[128,448]{0,1:T(8,128)(2,1)S(1)}, bf16[128,448]{0,1:T(8,128)(2,1)}, u32[]{:S(2)}) copy-start(bf16[128,448]{0,1:T(8,128)(2,1)} %param.10) | copy-start | bytes 344068
  17.6 33.7 %copy-start.1 = (bf16[7168,128]{1,0:T(8,128)(2,1)S(1)}, bf16[7168,128]{1,0:T(8,128)(2,1)}, u32[]{:S(2)}) copy-start(bf16[7168,128]{1,0:T(8,128)(2,1)} %get-tuple-element.8) | copy-start | bytes 5505028
  51.3 59.6 %copy-start.4 = (bf16[7168,128]{1,0:T(8,128)(2,1)S(1)}, bf16[7168,128]{1,0:T(8,128)(2,1)}, u32[]{:S(2)}) copy-start(bf16[7168,128]{1,0:T(8,128)(2,1)} %get-tuple-element.9) | copy-start | bytes 5505028
  162.7 5.4 %copy-start.5 = (s32[128,8]{0,1:T(8,128)S(1)}, s32[128,8]{0,1:T(8,128)}, u32[]{:S(2)}) copy-start(s32[128,8]{0,1:T(8,128)} %param.11) | copy-start | bytes 12292
  162.7 51.5 %all-to-all-start.8 = ((bf16[32,224,128]{2,1,0:T(8,128)(2,1)}), bf16[32,224,128]{2,1,0:T(8,128)(2,1)}, u32[]{:S(2)}, u32[]{:S(2)}) async-start(bf16[32,224,128]{2,1,0:T(8,128)(2,1)} %bitcast.36), calls=%async_computation.9 | async-start | bytes 3670016 | tf_op jit(solution)/shard_map/all_to_all | solution.py:110
  170.5 48.3 %copy-start.7 = (s32[32]{0:T(128)S(1)}, s32[32]{0:T(128)}, u32[]{:S(2)}) copy-start(s32[32]{0:T(128)} %param.13) | copy-start | bytes 388
  214.2 38.5 %all-to-all-start = ((bf16[32,40,448]{2,1,0:T(8,128)(2,1)}), bf16[32,40,448]{2,1,0:T(8,128)(2,1)S(1)}, u32[]{:S(2)}, u32[]{:S(2)}) async-start(bf16[32,40,448]{2,1,0:T(8,128)(2,1)} %bitcast.2), calls=%async_computation | async-start | bytes 2621440 | tf_op jit(solution)/shard_map/all_to_all | solution.py:110
  224.5 3.6 copy-start.2
  252.8 1.1 copy-start.3
  253.8 63.0 %all-to-all-start.5 = ((bf16[32,224,128]{2,1,0:T(8,128)(2,1)}), bf16[32,224,128]{2,1,0:T(8,128)(2,1)S(1)}, u32[]{:S(2)}, u32[]{:S(2)}) async-start(bf16[32,224,128]{2,1,0:T(8,128)(2,1)} %get-tuple-element.15), calls=%async_computation.6 | async-start | bytes 3670016 | tf_op jit(solution)/shard_map/all_to_all | solution.py:110
  260.1 86.5 %reduce-scatter.2.cloned.1.call-start = ((), (), s32[]{:S(2)}) async-start(), calls=%async_computation.11 | async-start | bytes 2949120 | tf_op jit(solution)/shard_map/reduce_scatter | solution.py:149
  316.8 58.4 %all-to-all-start.7 = ((bf16[32,224,128]{2,1,0:T(8,128)(2,1)}), bf16[32,224,128]{2,1,0:T(8,128)(2,1)}, u32[]{:S(2)}, u32[]{:S(2)}) async-start(bf16[32,224,128]{2,1,0:T(8,128)(2,1)} %get-tuple-element.14), calls=%async_computation.8 | async-start | bytes 3670016 | tf_op jit(solution)/shard_map/all_to_all | solution.py:110
  322.0 98.0 %all-gather.2.cloned.1.call-start = ((), (), s32[]{:S(2)}) async-start(), calls=%async_computation.12 | async-start | bytes 2949120 | tf_op jit(solution)/shard_map/all_gather | solution.py:151
  375.2 61.3 %all-to-all-start.9 = ((bf16[32,224,128]{2,1,0:T(8,128)(2,1)}), bf16[32,224,128]{2,1,0:T(8,128)(2,1)}, u32[]{:S(2)}, u32[]{:S(2)}) async-start(bf16[32,224,128]{2,1,0:T(8,128)(2,1)} %get-tuple-element.13), calls=%async_computation.10 | async-start | bytes 3670016 | tf_op jit(solution)/shard_map/all_to_all | solution.py:110
  426.4 14.4 %copy-start.6 = (f32[128,8]{0,1:T(8,128)S(1)}, f32[128,8]{0,1:T(8,128)}, u32[]{:S(2)}) copy-start(f32[128,8]{0,1:T(8,128)} %param.12) | copy-start | bytes 12292
  436.4 32.8 %all-to-all-start.3 = ((bf16[32,40,448]{2,1,0:T(8,128)(2,1)}), bf16[32,40,448]{2,1,0:T(8,128)(2,1)S(1)}, u32[]{:S(2)}, u32[]{:S(2)}) async-start(bf16[32,40,448]{2,1,0:T(8,128)(2,1)} %bitcast.29), calls=%async_computation.4 | async-start | bytes 2621440 | tf_op jit(solution)/shard_map/all_to_all | solution.py:110
Sparse Core Ops, SparseCore 0:
  266.8 79.8 reduce-scatter.1
  349.0 70.8 all-gather.1

commit v2 on v1

v2 whole, which is shorter than its diff:
```python
import functools

import jax
import jax.numpy as jnp
from jax import lax
from jax.experimental import pallas as pl
from jax.experimental.pallas import tpu as pltpu
from jax.sharding import PartitionSpec as P

beta_first = 0.9
beta_second = 0.95
learning_rate = 0.003
weight_decay = 0.1
epsilon = 1e-08

Y, Z, CORE = 4, 4, 2
PAIR, X = 2, 4


def expert_index(y, z, core):
    return (y % Y) * (Z * CORE) + (z % Z) * CORE + core


def shift(array, dy=0, dz=0, dcore=0, dpair=0, dx=0):
    if not (dy % Y or dz % Z or dcore or dpair or dx % X):
        return array
    sites = [
        (y, z, core, pair, x)
        for y in range(Y)
        for z in range(Z)
        for core in range(CORE)
        for pair in range(PAIR)
        for x in range(X)
    ]

    def index(y, z, core, pair, x):
        return expert_index(y, z, core) * (PAIR * X) + pair * X + x % X

    pairs = [
        (index(*site), index(site[0] + dy, site[1] + dz, site[2] ^ dcore, site[3] ^ dpair, site[4] + dx))
        for site in sites
    ]
    return lax.ppermute(array, ("expert", "cuts"), pairs)


def adamw_kernel(weights, grads, first, second, out):
    gradient = grads[...].astype(jnp.float32)
    first_new = beta_first * first[...].astype(jnp.float32) + (1.0 - beta_first) * gradient
    second_new = (
        beta_second * second[...].astype(jnp.float32)
        + (1.0 - beta_second) * gradient * gradient
    )
    current = weights[...].astype(jnp.float32)
    root = second_new * lax.rsqrt(second_new)
    updated = current - learning_rate * (first_new / (root + epsilon) + weight_decay * current)
    for place, array in enumerate((updated, first_new, second_new)):
        out[:, place] = array.astype(jnp.bfloat16)


def adamw(weights, grads, first, second, steps):
    chunks, rows, lanes = weights.shape
    block = pl.BlockSpec((chunks // steps, rows, lanes), lambda i: (i, 0, 0))
    elements = chunks * rows * lanes
    return pl.pallas_call(
        adamw_kernel,
        grid=(steps,),
        in_specs=[block] * 4,
        out_specs=pl.BlockSpec((chunks // steps, 3, rows, lanes), lambda i: (i, 0, 0, 0)),
        out_shape=jax.ShapeDtypeStruct((chunks, 3, rows, lanes), jnp.bfloat16),
        cost_estimate=pl.CostEstimate(
            flops=12 * elements, bytes_accessed=14 * elements, transcendentals=elements
        ),
        name="adamw",
    )(weights, grads, first, second)


def order_kernel(array, *refs):
    pass


def after(array, *earlier):
    anywhere = pl.BlockSpec(memory_space=pl.ANY)
    return pl.pallas_call(
        order_kernel,
        in_specs=[anywhere] * (1 + len(earlier)),
        out_specs=anywhere,
        out_shape=jax.ShapeDtypeStruct(array.shape, array.dtype),
        input_output_aliases={0: 0},
        cost_estimate=pl.CostEstimate(flops=0, bytes_accessed=0, transcendentals=0),
        name="after",
    )(array, *earlier)


def exchange(array):
    return lax.all_to_all(array, "expert", split_axis=0, concat_axis=0, tiled=True)


def whole(kernel, inputs, shapes, flops, name, scratch=()):
    sizes = [array.size * array.dtype.itemsize for array in (*inputs, *shapes)]
    vmem = pl.BlockSpec(memory_space=pltpu.VMEM)
    return pl.pallas_call(
        kernel,
        in_specs=[vmem] * len(inputs),
        out_specs=[vmem] * len(shapes),
        out_shape=shapes,
        scratch_shapes=scratch,
        compiler_params=pltpu.CompilerParams(vmem_limit_bytes=40 * 2**20),
        cost_estimate=pl.CostEstimate(flops=flops, bytes_accessed=sum(sizes), transcendentals=0),
        name=name,
    )(*inputs)


def dispatch_kernel(slot, tokens, *outs):
    for place in range(slot.shape[0]):
        out = outs[place % Y].at[place // Y]
        rows = lax.broadcasted_iota(jnp.int32, (out.shape[0], slot.shape[1]), 0)
        chosen = jnp.where(slot[place : place + 1, :] == rows, 1.0, 0.0).astype(jnp.bfloat16)
        out[...] = jnp.dot(chosen, tokens[...], preferred_element_type=jnp.float32).astype(
            jnp.bfloat16
        )


def dispatch(slot, tokens, rows):
    shape = jax.ShapeDtypeStruct((CORE, rows, tokens.shape[1]), jnp.bfloat16)
    flops = 200 * slot.shape[0] * rows * tokens.size
    return whole(dispatch_kernel, [slot, tokens], [shape] * Y, flops, "dispatch")


def plane_shift(parts, sign, earlier=()):
    arrived = [shift(part, dy=sign * dy) for dy, part in enumerate(parts)]
    swapped = jnp.stack([part[1] for part in arrived])
    if earlier:
        swapped = after(swapped, *earlier)
    return [*arrived, shift(swapped, dcore=1)]


def rows_of(refs):
    return [ref.at[0] for ref in refs[:Y]] + [refs[Y].at[dy] for dy in range(Y)]


def up_kernel(*refs):
    rows, blocks = rows_of(refs), refs[Y + 1 : Y + 1 + X]
    outs, joined = refs[Y + 1 + X : -1], refs[-1]
    width = outs[0].shape[1]
    for number, block in enumerate(blocks):
        joined[:, number * width : (number + 1) * width] = block[...]
    for place, part in enumerate(rows):
        count = part.shape[0]
        product = jnp.dot(part[...], joined[...], preferred_element_type=jnp.float32)
        for number, out in enumerate(outs):
            out[place * count : (place + 1) * count, :] = product[
                :, number * width : (number + 1) * width
            ].astype(jnp.bfloat16)


def up_project(rows, blocks):
    features, width = blocks[0].shape
    count = Y * CORE * rows[0].shape[1]
    return whole(
        up_kernel,
        [*rows, *blocks],
        [jax.ShapeDtypeStruct((count, width), jnp.bfloat16)] * len(blocks),
        2 * count * features * width * len(blocks),
        "up_project",
        [pltpu.VMEM((features, len(blocks) * width), jnp.bfloat16)],
    )


def down_kernel(*refs):
    hidden, blocks, outs, joined = refs[:X], refs[X : 2 * X], refs[2 * X : -1], refs[-1]
    width = hidden[0].shape[1]
    for number, block in enumerate(blocks):
        joined[:, number * width : (number + 1) * width] = block[...]
    for place in range(Y * CORE):
        out = outs[place % Y].at[place // Y]
        count = out.shape[0]
        rows = jnp.concatenate(
            [part[place * count : (place + 1) * count, :] for part in hidden], axis=1
        )
        out[...] = lax.dot_general(
            rows, joined[...], (((1,), (1,)), ((), ())), preferred_element_type=jnp.float32
        ).astype(jnp.bfloat16)


def down_project(hidden, blocks):
    features, width = blocks[0].shape
    count = hidden[0].shape[0]
    return whole(
        down_kernel,
        [*hidden, *blocks],
        [jax.ShapeDtypeStruct((CORE, count // (Y * CORE), features), jnp.bfloat16)] * Y,
        2 * count * features * width * len(blocks),
        "down_project",
        [pltpu.VMEM((features, len(blocks) * width), jnp.bfloat16)],
    )


def combine_kernel(slot, high, low, *refs):
    outputs, out = rows_of(refs), refs[-1]
    total = jnp.zeros(out.shape, jnp.float32)
    for place, part in enumerate(outputs):
        rows = lax.broadcasted_iota(jnp.int32, (part.shape[0], slot.shape[1]), 0)
        found = slot[place : place + 1, :] == rows
        for gate in (high, low):
            share = jnp.where(found, gate[place : place + 1, :], 0.0).astype(jnp.bfloat16)
            total += lax.dot_general(
                share, part[...], (((0,), (0,)), ((), ())), preferred_element_type=jnp.float32
            )
    out[...] = total


def combine(slot, high, low, outputs):
    tokens, features = slot.shape[1], outputs[0].shape[2]
    flops = 4 * slot.size * outputs[0].shape[1] * features
    shape = jax.ShapeDtypeStruct((tokens, features), jnp.float32)
    return whole(combine_kernel, [slot, high, low, *outputs], [shape], flops, "combine")[0]


def local(tokens, routing, gate_weights, owner, weights, grads, first, second):
    expert_count = owner.shape[0]
    cut_count = lax.axis_size("cuts")
    token_count, features = tokens.shape
    top_count = routing.shape[1]
    capacity = 5 * token_count * top_count // (4 * expert_count)
    state_shape = weights.shape
    width = state_shape[3]
    me = lax.axis_index("expert")
    my_y, my_z, my_core = me // (Z * CORE), (me // CORE) % Z, me % CORE
    cut = lax.axis_index("cuts")
    my_pair, my_x = cut // X, cut % X
    plane = [(dcore, dy) for dcore in range(CORE) for dy in range(Y)]
    pieces = [
        array.reshape(expert_count, -1, width) for array in (weights, grads, first, second)
    ]
    state = adamw(*pieces, 8)
    order = jnp.arange(expert_count, dtype=jnp.int32)
    matches = routing[:, None, :] == order[None, :, None]
    gate = jnp.sum(jnp.where(matches, gate_weights[:, None, :], 0.0), axis=2)
    gate = jnp.where(jnp.any(matches, axis=2), gate, -1.0)
    high = gate.astype(jnp.bfloat16)
    low = (gate - high.astype(jnp.float32)).astype(jnp.bfloat16)
    wide = jnp.concatenate([tokens, shift(tokens, dpair=1), high, low], axis=1)
    near = [shift(wide, dz=dz) for dz in range(Z)]
    spread = exchange(state)
    near = jnp.concatenate(near, axis=0)
    gates = near[:, 2 * features :].T.astype(jnp.float32)
    gates = gates.reshape(2, Y, Z, CORE, Z * token_count)
    gates = lax.dynamic_index_in_dim(gates, my_z, axis=2, keepdims=False)
    high, low = (
        jnp.stack(
            [
                lax.dynamic_slice(
                    part, ((my_y + dy) % Y, my_core ^ dcore, 0), (1, 1, Z * token_count)
                )[0, 0]
                for dcore, dy in plane
            ]
        )
        for part in gates
    )
    near = near[:, : 2 * features]

    positions = jnp.arange(token_count, dtype=jnp.int32)
    earlier = (positions[:, None] < positions[None, :]).astype(jnp.bfloat16)
    named = (high >= 0.0).reshape(len(plane) * Z, token_count)
    slot = jnp.dot(
        named.astype(jnp.bfloat16), earlier, preferred_element_type=jnp.float32
    ).astype(jnp.int32)
    slot = slot + capacity * (jnp.arange(len(plane) * Z, dtype=jnp.int32) % Z)[:, None]
    slot = jnp.where(named, slot, -1).reshape(len(plane), Z * token_count)
    buffered = dispatch(slot, near, Z * capacity)

    by_cut = state[:, 0].reshape(2, cut_count, features, width)
    blocks = []
    for dx in range(X):
        block = jnp.concatenate(
            [
                lax.dynamic_slice_in_dim(by_cut, pair * X + (my_x + dx) % X, 1, axis=1)[:, 0]
                for pair in (my_pair, my_pair ^ 1)
            ],
            axis=1,
        )
        blocks.append(shift(block, dx=dx))

    incoming = plane_shift(buffered, 1, blocks)

    parts = up_project(incoming, [block[0] for block in blocks])
    total = sum(shift(part, dx=-dx).astype(jnp.float32) for dx, part in enumerate(parts))
    hidden = jax.nn.silu(total).astype(jnp.bfloat16)

    every = [shift(hidden, dx=dx) for dx in range(X)]
    expert_out = down_project(every, [block[1] for block in blocks])

    holder = jnp.sum(order[None, :] * (owner[None, :] == order[:, None]), axis=1)
    arrived = exchange(after(jnp.take(spread, holder, axis=0, mode="clip"), expert_out[0]))

    returned = plane_shift(expert_out, -1)

    partial = combine(slot, high, low, returned)
    partial = partial.astype(jnp.bfloat16).reshape(Z, token_count, PAIR, features)
    moved = [arrived[:, place].reshape(state_shape) for place in range(3)]
    mixed = sum(
        shift(partial[dz, :, dpair], dz=-dz, dpair=dpair).astype(jnp.float32)
        for dz in range(Z)
        for dpair in range(PAIR)
        if dz or dpair
    )
    mixed += after(partial[0, :, 0], *moved).astype(jnp.float32)
    return (mixed.astype(jnp.bfloat16), *moved)


def solution(mesh):
    state = P("expert", None, None, "cuts")
    return jax.shard_map(
        local,
        mesh=mesh,
        in_specs=(
            P("expert", "cuts"),
            P("expert", None),
            P("expert", None),
            P(),
            state,
            state,
            state,
            state,
        ),
        out_specs=(P("expert", "cuts"), state, state, state),
        check_vma=False,
    )
```

time: 492 us -> 325 us (0.66)
  blocking collectives: 145 us -> 0 us
  waiting for transfers between devices: 243 us -> 185 us
  starting transfers between devices: 30.5 us -> 83.5 us
  between operations: 14.2 us -> 1.15 us
  local copies, waits for them, and re-layouts: 20.3 us -> 25.8 us
    ppermute x0 -> x28, waiting for transfers between devices: none -> 185 us  [shift(): return lax.ppermute(array, ('expert', 'cuts'), pairs)]
    all_to_all x6 -> x2, waiting for transfers between devices: 179 us -> 0.01 us  [exchange(): lax.all_to_all(array, 'expert', split_axis=0, concat_axis=0, tiled=True)]
    all_to_all x4 -> x0, blocking collectives: 145 us -> none  [exchange(): return lax.all_to_all(array, axis, split_axis=0, concat_axis=0, tiled=True)]
    ppermute x0 -> x28, starting transfers between devices: none -> 65.3 us  [shift(): return lax.ppermute(array, ('expert', 'cuts'), pairs)]
    all_gather x1 -> x0, waiting for transfers between devices: 40 us -> none  [local(): every = lax.all_gather(hidden, 'cuts', axis=0, tiled=False)]
    reduce_scatter x1 -> x0, waiting for transfers between devices: 24.6 us -> none  [local(): lax.psum_scatter(parts, 'cuts', scatter_dimension=0, tiled=False)]
    all_to_all x6 -> x2, starting transfers between devices: 30.5 us -> 18.2 us  [exchange(): lax.all_to_all(array, 'expert', split_axis=0, concat_axis=0, tiled=True)]
    slice x1 -> x11, local copies, waits for them, and re-layouts: 1.57 us -> 9.78 us  [the longest x1 5.17 us: local(): moved = [arrived[:, place].reshape(state_shape) for place in range(3)]]
  transfers between devices with their start and end apart: 8 -> 30, of which waited for: 8 -> 15; matrix products, arithmetic and copies ran while one was open for 4% -> 7% of each run, Pallas kernels for 3% -> 6%
where the time goes in v2:
time: 325 us; the launch traced here: 322 us
  waiting for transfers between devices  185 us (57%)
  starting transfers between devices  83.5 us (26%)
  local copies, waits for them, and re-layouts  25.8 us (8%)
  Pallas kernels  20.2 us (6%)
  other arithmetic  6.73 us (2%)
    ppermute x28, waiting for transfers between devices, shift(): return lax.ppermute(array, ('expert', 'cuts'), pairs)  185 us
    ppermute x28, starting transfers between devices, shift(): return lax.ppermute(array, ('expert', 'cuts'), pairs)  65.3 us
    all_to_all x2, starting transfers between devices, exchange(): lax.all_to_all(array, 'expert', split_axis=0, concat_axis=0, tiled=True)  18.2 us
    pallas_call x4, Pallas kernels, whole(): pl.pallas_call(kernel, in_specs=[vmem] * len(inputs), out_specs=[vmem] *...  10.9 us
    pallas_call x1, Pallas kernels, adamw(): pl.pallas_call(adamw_kernel, grid=(steps,), in_specs=[block] * 4, out_spe...  9.29 us
  transfers between devices with their start and end apart: 30, of which 15 were waited for; matrix products, arithmetic and copies ran while one was open for 7% of the time, Pallas kernels for 6%

profile of v2, /device:TPU:1, one launch (start us, length us, event | category | flops | bytes accessed | tf_op | source)
XLA Modules:
  0.0 322.1 jit_solution(18313321229566159214)
XLA Ops:
  1.6 2.6 collective-permute-start
  6.7 3.8 %collective-permute-start.1 = (bf16[128,960]{1,0:T(8,128)(2,1)S(1)}, bf16[128,960]{1,0:T(8,128)(2,1)S(1)}, u32[]{:S(2)}, u32[]{:S(2)}) collective-permute-start(bf16[128,960]{1,0:T(8,128)(2,1)S(1)} %pad_maximum_fusion.12), channel_id=1, source_target_pairs={{0,16},{1,17},{2,18},{3,19},{4,20},{5,21},{6,22},{7,23},{8,24},{9,... | collective-permute-start | bytes 737288 | tf_op jit(solution)/shard_map/ppermute | solution.py:43
  10.5 4.7 %collective-permute-start.2 = (bf16[128,960]{1,0:T(8,128)(2,1)S(1)}, bf16[128,960]{1,0:T(8,128)(2,1)S(1)}, u32[]{:S(2)}, u32[]{:S(2)}) collective-permute-start(bf16[128,960]{1,0:T(8,128)(2,1)S(1)} %pad_maximum_fusion.12), channel_id=1, source_target_pairs={{0,32},{1,33},{2,34},{3,35},{4,36},{5,37},{6,38},{7,39},{8,40},{9,... | collective-permute-start | bytes 737288 | tf_op jit(solution)/shard_map/ppermute | solution.py:43
  17.6 9.3 %adamw.1 = bf16[32,3,224,128]{3,2,1,0:T(8,128)(2,1)} custom-call(bf16[32,224,128]{2,1,0:T(8,128)(2,1)} %bitcast.122, bf16[32,224,128]{2,1,0:T(8,128)(2,1)} %bitcast.123, bf16[32,224,128]{2,1,0:T(8,128)(2,1)} %bitcast.124, bf16[32,224,128]{2,1,0:T(8,128)(2,1)} %bitcast.125), custom_call_target="tpu_custom_call" | custom-call | flops 11010048 | bytes 12845056 | tf_op jit(solution)/shard_map/adamw/pallas_call | solution.py:64
  26.9 7.5 %all-to-all-start = ((bf16[32,3,224,128]{3,2,1,0:T(8,128)(2,1)}), bf16[32,3,224,128]{3,2,1,0:T(8,128)(2,1)}, u32[]{:S(2)}, u32[]{:S(2)}) async-start(bf16[32,3,224,128]{3,2,1,0:T(8,128)(2,1)} %adamw.1), calls=%async_computation | async-start | bytes 11010048 | tf_op jit(solution)/shard_map/all_to_all | solution.py:95
  34.6 4.5 %collective-permute-done.3 = bf16[128,960]{1,0:T(8,128)(2,1)S(1)} collective-permute-done((bf16[128,960]{1,0:T(8,128)(2,1)S(1)}, bf16[128,960]{1,0:T(8,128)(2,1)S(1)}, u32[]{:S(2)}, u32[]{:S(2)}) %collective-permute-start.3) | collective-permute-done | bytes 245792 | tf_op jit(solution)/shard_map/ppermute | solution.py:43
  43.1 2.8 slice.127
  47.6 2.8 collective-permute-start.5
  51.4 2.6 collective-permute-start.9
  54.7 41.7 %collective-permute-done.4.refs_1_ = bf16[2,160,896]{2,1,0:T(8,128)(2,1)S(1)} collective-permute-done((bf16[2,160,896]{2,1,0:T(8,128)(2,1)}, bf16[2,160,896]{2,1,0:T(8,128)(2,1)S(1)}, u32[]{:S(2)}, u32[]{:S(2)}) %collective-permute-start.4) | collective-permute-done | bytes 573472 | tf_op jit(solution)/shard_map/ppermute | solution.py:43
  98.4 16.3 %collective-permute-done.5.refs_2_ = bf16[2,160,896]{2,1,0:T(8,128)(2,1)S(1)} collective-permute-done((bf16[2,160,896]{2,1,0:T(8,128)(2,1)S(1)}, bf16[2,160,896]{2,1,0:T(8,128)(2,1)S(1)}, u32[]{:S(2)}, u32[]{:S(2)}) %collective-permute-start.5) | collective-permute-done | bytes 573472 | tf_op jit(solution)/shard_map/ppermute | solution.py:43
  125.9 6.0 %collective-permute-done.11 = bf16[1280,128]{1,0:T(8,128)(2,1)S(1)} collective-permute-done((bf16[1280,128]{1,0:T(8,128)(2,1)S(1)}, bf16[1280,128]{1,0:T(8,128)(2,1)S(1)}, u32[]{:S(2)}, u32[]{:S(2)}) %collective-permute-start.11) | collective-permute-done | bytes 327712 | tf_op jit(solution)/shard_map/ppermute | solution.py:43
  131.8 2.6 collective-permute-done.12
  134.5 8.5 %collective-permute-done.13 = bf16[1280,128]{1,0:T(8,128)(2,1)S(1)} collective-permute-done((bf16[1280,128]{1,0:T(8,128)(2,1)S(1)}, bf16[1280,128]{1,0:T(8,128)(2,1)S(1)}, u32[]{:S(2)}, u32[]{:S(2)}) %collective-permute-start.13) | collective-permute-done | bytes 327712 | tf_op jit(solution)/shard_map/ppermute | solution.py:43
  146.2 14.3 %collective-permute-done.14.refs_1_ = bf16[1280,128]{1,0:T(8,128)(2,1)S(1)} collective-permute-done((bf16[1280,128]{1,0:T(8,128)(2,1)S(1)}, bf16[1280,128]{1,0:T(8,128)(2,1)S(1)}, u32[]{:S(2)}, u32[]{:S(2)}) %collective-permute-start.14) | collective-permute-done | bytes 327712 | tf_op jit(solution)/shard_map/ppermute | solution.py:43
  160.9 2.7 down_project.1
  164.3 6.3 %gather_fusion = bf16[32,3,224,128]{3,2,1,0:T(8,128)(2,1)} fusion(bf16[32,3,224,128]{3,2,1,0:T(8,128)(2,1)} %all-to-all-done, s32[1024]{0:T(1024)S(1)} %pad_clamp_fusion), kind=kCustom, calls=%fused_computation | custom fusion | bytes 11010176 | tf_op jit(solution)/shard_map/jit(_take)/gather | solution.py:294
  170.6 10.7 %all-to-all-start.1 = ((bf16[32,3,224,128]{3,2,1,0:T(8,128)(2,1)}), bf16[32,3,224,128]{3,2,1,0:T(8,128)(2,1)}, u32[]{:S(2)}, u32[]{:S(2)}) async-start(bf16[32,3,224,128]{3,2,1,0:T(8,128)(2,1)} %after.4), calls=%async_computation.1 | async-start | bytes 11010048 | tf_op jit(solution)/shard_map/all_to_all | solution.py:95
  181.3 2.7 collective-permute-start.17
  185.2 28.0 %collective-permute-done.17.refs_1_ = bf16[2,160,896]{2,1,0:T(8,128)(2,1)S(1)} collective-permute-done((bf16[2,160,896]{2,1,0:T(8,128)(2,1)}, bf16[2,160,896]{2,1,0:T(8,128)(2,1)S(1)}, u32[]{:S(2)}, u32[]{:S(2)}) %collective-permute-start.17) | collective-permute-done | bytes 573472 | tf_op jit(solution)/shard_map/ppermute | solution.py:43
  213.3 6.9 %collective-permute-done.18.refs_2_ = bf16[2,160,896]{2,1,0:T(8,128)(2,1)S(1)} collective-permute-done((bf16[2,160,896]{2,1,0:T(8,128)(2,1)S(1)}, bf16[2,160,896]{2,1,0:T(8,128)(2,1)S(1)}, u32[]{:S(2)}, u32[]{:S(2)}) %collective-permute-start.18) | collective-permute-done | bytes 573472 | tf_op jit(solution)/shard_map/ppermute | solution.py:43
  220.2 20.3 %collective-permute-done.19.refs_3_ = bf16[2,160,896]{2,1,0:T(8,128)(2,1)S(1)} collective-permute-done((bf16[2,160,896]{2,1,0:T(8,128)(2,1)S(1)}, bf16[2,160,896]{2,1,0:T(8,128)(2,1)S(1)}, u32[]{:S(2)}, u32[]{:S(2)}) %collective-permute-start.19) | collective-permute-done | bytes 573472 | tf_op jit(solution)/shard_map/ppermute | solution.py:43
  242.5 2.6 collective-permute-done.20.refs_4_
  245.1 4.6 %combine.1 = f32[512,896]{1,0:T(8,128)S(1)} custom-call(s32[8,512]{1,0:T(8,128)S(1)} %reshape.88.slot, f32[8,512]{1,0:T(8,128)S(1)} %stack.12.high, f32[8,512]{1,0:T(8,128)S(1)} %stack.13.low, bf16[2,160,896]{2,1,0:T(8,128)(2,1)S(1)} %copy-done.1, bf16[2,160,896]{2,1,0:T(8,128)(2,1)S(1)} %collective-permute-done.17.refs_1_, ...), custom_call_target="tpu_custom_call" | custom-call | flops 2348810240 | bytes 5324800 | tf_op jit(solution)/shard_map/combine/pallas_call | solution.py:101
  252.3 12.8 %collective-permute-start.21 = (bf16[128,448]{1,0:T(8,128)(2,1)S(1)}, bf16[128,448]{1,0:T(8,128)(2,1)S(1)}, u32[]{:S(2)}, u32[]{:S(2)}) collective-permute-start(bf16[128,448]{1,0:T(8,128)(2,1)S(1)} %bitcast.133), channel_id=1, source_target_pairs={{0,4},{1,5},{2,6},{3,7},{4,0},{5,1},{6,2},{7,3},{8,12},{9,13},{10,... | collective-permute-start | bytes 344072 | tf_op jit(solution)/shard_map/ppermute | solution.py:43
  265.2 3.0 collective-permute-start.22
  268.9 2.9 collective-permute-start.23
  272.8 5.7 %collective-permute-start.25 = (bf16[128,448]{1,0:T(8,128)(2,1)S(1)}, bf16[128,448]{1,0:T(8,128)(2,1)S(1)}, u32[]{:S(2)}, u32[]{:S(2)}) collective-permute-start(bf16[128,448]{1,0:T(8,128)(2,1)S(1)} %bitcast.129), channel_id=1, source_target_pairs={{0,36},{1,37},{2,38},{3,39},{4,32},{5,33},{6,34},{7,35},{8,44},{9,... | collective-permute-start | bytes 344072 | tf_op jit(solution)/shard_map/ppermute | solution.py:43
  278.6 27.4 %collective-permute-done.21 = bf16[128,448]{1,0:T(8,128)(2,1)S(1)} collective-permute-done((bf16[128,448]{1,0:T(8,128)(2,1)S(1)}, bf16[128,448]{1,0:T(8,128)(2,1)S(1)}, u32[]{:S(2)}, u32[]{:S(2)}) %collective-permute-start.21) | collective-permute-done | bytes 114720 | tf_op jit(solution)/shard_map/ppermute | solution.py:43
  305.9 4.6 %collective-permute-start.27 = (bf16[128,448]{1,0:T(8,128)(2,1)S(1)}, bf16[128,448]{1,0:T(8,128)(2,1)S(1)}, u32[]{:S(2)}, u32[]{:S(2)}) collective-permute-start(bf16[128,448]{1,0:T(8,128)(2,1)S(1)} %bitcast.130), channel_id=1, source_target_pairs={{0,20},{1,21},{2,22},{3,23},{4,16},{5,17},{6,18},{7,19},{8,28},{9,... | collective-permute-start | bytes 344072 | tf_op jit(solution)/shard_map/ppermute | solution.py:43
  310.6 5.2 %fusion.24 = (bf16[32,1,224,128]{3,2,1,0:T(8,128)(2,1)}, bf16[32,1,224,128]{3,2,1,0:T(8,128)(2,1)}, bf16[32,1,224,128]{3,2,1,0:T(8,128)(2,1)}) fusion(bf16[32,3,224,128]{3,2,1,0:T(8,128)(2,1)} %all-to-all-done.1), kind=kLoop, calls=%fused_computation.94 | loop fusion | bytes 11010048 | tf_op jit(solution)/shard_map/slice | solution.py:300
  315.8 4.5 %collective-permute-done.27 = bf16[128,448]{1,0:T(8,128)(2,1)S(1)} collective-permute-done((bf16[128,448]{1,0:T(8,128)(2,1)S(1)}, bf16[128,448]{1,0:T(8,128)(2,1)S(1)}, u32[]{:S(2)}, u32[]{:S(2)}) %collective-permute-start.27) | collective-permute-done | bytes 114720 | tf_op jit(solution)/shard_map/ppermute | solution.py:43
  (108 shorter events, 40.0 us)
Async XLA Ops:
  1.6 4.9 %collective-permute-start = (bf16[128,448]{1,0:T(8,128)(2,1)S(1)}, bf16[128,448]{1,0:T(8,128)(2,1)S(1)}, u32[]{:S(2)}, u32[]{:S(2)}) collective-permute-start(bf16[128,448]{1,0:T(8,128)(2,1)S(1)} %copy.77), channel_id=1, source_target_pairs={{0,4},{1,5},{2,6},{3,7},{4,0},{5,1},{6,2},{7,3},{8,12},{9,13},{10,... | collective-permute-start | bytes 344072 | tf_op jit(solution)/shard_map/ppermute | solution.py:43
  6.7 27.9 %collective-permute-start.1 = (bf16[128,960]{1,0:T(8,128)(2,1)S(1)}, bf16[128,960]{1,0:T(8,128)(2,1)S(1)}, u32[]{:S(2)}, u32[]{:S(2)}) collective-permute-start(bf16[128,960]{1,0:T(8,128)(2,1)S(1)} %pad_maximum_fusion.12), channel_id=1, source_target_pairs={{0,16},{1,17},{2,18},{3,19},{4,20},{5,21},{6,22},{7,23},{8,24},{9,... | collective-permute-start | bytes 737288 | tf_op jit(solution)/shard_map/ppermute | solution.py:43
  10.5 24.1 %collective-permute-start.2 = (bf16[128,960]{1,0:T(8,128)(2,1)S(1)}, bf16[128,960]{1,0:T(8,128)(2,1)S(1)}, u32[]{:S(2)}, u32[]{:S(2)}) collective-permute-start(bf16[128,960]{1,0:T(8,128)(2,1)S(1)} %pad_maximum_fusion.12), channel_id=1, source_target_pairs={{0,32},{1,33},{2,34},{3,35},{4,36},{5,37},{6,38},{7,39},{8,40},{9,... | collective-permute-start | bytes 737288 | tf_op jit(solution)/shard_map/ppermute | solution.py:43
  15.2 23.9 %collective-permute-start.3 = (bf16[128,960]{1,0:T(8,128)(2,1)S(1)}, bf16[128,960]{1,0:T(8,128)(2,1)S(1)}, u32[]{:S(2)}, u32[]{:S(2)}) collective-permute-start(bf16[128,960]{1,0:T(8,128)(2,1)S(1)} %pad_maximum_fusion.12), channel_id=1, source_target_pairs={{0,48},{1,49},{2,50},{3,51},{4,52},{5,53},{6,54},{7,55},{8,56},{9,... | collective-permute-start | bytes 737288 | tf_op jit(solution)/shard_map/ppermute | solution.py:43
  26.9 137.4 %all-to-all-start = ((bf16[32,3,224,128]{3,2,1,0:T(8,128)(2,1)}), bf16[32,3,224,128]{3,2,1,0:T(8,128)(2,1)}, u32[]{:S(2)}, u32[]{:S(2)}) async-start(bf16[32,3,224,128]{3,2,1,0:T(8,128)(2,1)} %adamw.1), calls=%async_computation | async-start | bytes 11010048 | tf_op jit(solution)/shard_map/all_to_all | solution.py:95
  41.9 54.5 %collective-permute-start.4 = (bf16[2,160,896]{2,1,0:T(8,128)(2,1)}, bf16[2,160,896]{2,1,0:T(8,128)(2,1)S(1)}, u32[]{:S(2)}, u32[]{:S(2)}) collective-permute-start(bf16[2,160,896]{2,1,0:T(8,128)(2,1)} %get-tuple-element.17), channel_id=1, source_target_pairs={{0,64},{1,65},{2,66},{3,67},{4,68},{5,69},{6,70},{7,71},{8,72},{9,... | collective-permute-start | bytes 1720328 | tf_op jit(solution)/shard_map/ppermute | solution.py:43
  47.6 50.8 %copy-start.2 = (bf16[2,448,128]{2,1,0:T(8,128)(2,1)}, bf16[2,448,128]{2,1,0:T(8,128)(2,1)S(1)}, u32[]{:S(2)}) copy-start(bf16[2,448,128]{2,1,0:T(8,128)(2,1)S(1)} %get-tuple-element.52) | copy-start | bytes 688132
  47.6 50.8 %copy-start.4 = (bf16[2,448,128]{2,1,0:T(8,128)(2,1)}, bf16[2,448,128]{2,1,0:T(8,128)(2,1)S(1)}, u32[]{:S(2)}) copy-start(bf16[2,448,128]{2,1,0:T(8,128)(2,1)S(1)} %get-tuple-element.53) | copy-start | bytes 688132
  47.6 67.1 %collective-permute-start.5 = (bf16[2,160,896]{2,1,0:T(8,128)(2,1)S(1)}, bf16[2,160,896]{2,1,0:T(8,128)(2,1)S(1)}, u32[]{:S(2)}, u32[]{:S(2)}) collective-permute-start(bf16[2,160,896]{2,1,0:T(8,128)(2,1)S(1)} %get-tuple-element.18), channel_id=1, source_target_pairs={{0,128},{1,129},{2,130},{3,131},{4,132},{5,133},{6,134},{7,135},{8... | collective-permute-start | bytes 1720328 | tf_op jit(solution)/shard_map/ppermute | solution.py:43
  50.5 64.3 %collective-permute-start.6 = (bf16[2,160,896]{2,1,0:T(8,128)(2,1)S(1)}, bf16[2,160,896]{2,1,0:T(8,128)(2,1)S(1)}, u32[]{:S(2)}, u32[]{:S(2)}) collective-permute-start(bf16[2,160,896]{2,1,0:T(8,128)(2,1)S(1)} %get-tuple-element.19), channel_id=1, source_target_pairs={{0,192},{1,193},{2,194},{3,195},{4,196},{5,197},{6,198},{7,199},{8... | collective-permute-start | bytes 1720328 | tf_op jit(solution)/shard_map/ppermute | solution.py:43
  51.4 64.5 %collective-permute-start.9 = (bf16[2,896,128]{2,1,0:T(8,128)(2,1)S(1)}, bf16[2,896,128]{2,1,0:T(8,128)(2,1)}, u32[]{:S(2)}, u32[]{:S(2)}) collective-permute-start(bf16[2,896,128]{2,1,0:T(8,128)(2,1)S(1)} %pad_maximum_fusion.11), channel_id=1, source_target_pairs={{0,3},{1,0},{2,1},{3,2},{4,7},{5,4},{6,5},{7,6},{8,11},{9,8},{10,9... | collective-permute-start | bytes 1376264 | tf_op jit(solution)/shard_map/ppermute | solution.py:43
  54.0 61.9 %collective-permute-start.8 = (bf16[2,896,128]{2,1,0:T(8,128)(2,1)S(1)}, bf16[2,896,128]{2,1,0:T(8,128)(2,1)}, u32[]{:S(2)}, u32[]{:S(2)}) collective-permute-start(bf16[2,896,128]{2,1,0:T(8,128)(2,1)S(1)} %pad_maximum_fusion.10), channel_id=1, source_target_pairs={{0,2},{1,3},{2,0},{3,1},{4,6},{5,7},{6,4},{7,5},{8,10},{9,11},{10,... | collective-permute-start | bytes 1376264 | tf_op jit(solution)/shard_map/ppermute | solution.py:43
  96.4 19.6 %collective-permute-start.7 = (bf16[2,896,128]{2,1,0:T(8,128)(2,1)S(1)}, bf16[2,896,128]{2,1,0:T(8,128)(2,1)}, u32[]{:S(2)}, u32[]{:S(2)}) collective-permute-start(bf16[2,896,128]{2,1,0:T(8,128)(2,1)S(1)} %pad_maximum_fusion.9), channel_id=1, source_target_pairs={{0,1},{1,2},{2,3},{3,0},{4,5},{5,6},{6,7},{7,4},{8,9},{9,10},{10,1... | collective-permute-start | bytes 1376264 | tf_op jit(solution)/shard_map/ppermute | solution.py:43
  116.0 4.5 %collective-permute-start.10 = (bf16[4,160,896]{2,1,0:T(8,128)(2,1)}, bf16[4,160,896]{2,1,0:T(8,128)(2,1)S(1)}, u32[]{:S(2)}, u32[]{:S(2)}) collective-permute-start(bf16[4,160,896]{2,1,0:T(8,128)(2,1)} %after.3), channel_id=1, source_target_pairs={{0,8},{1,9},{2,10},{3,11},{4,12},{5,13},{6,14},{7,15},{8,0},{9,1},... | collective-permute-start | bytes 3440648 | tf_op jit(solution)/shard_map/ppermute | solution.py:43
  122.2 9.6 %collective-permute-start.11 = (bf16[1280,128]{1,0:T(8,128)(2,1)S(1)}, bf16[1280,128]{1,0:T(8,128)(2,1)S(1)}, u32[]{:S(2)}, u32[]{:S(2)}) collective-permute-start(bf16[1280,128]{1,0:T(8,128)(2,1)S(1)} %get-tuple-element.21), channel_id=1, source_target_pairs={{0,3},{1,0},{2,1},{3,2},{4,7},{5,4},{6,5},{7,6},{8,11},{9,8},{10,9... | collective-permute-start | bytes 983048 | tf_op jit(solution)/shard_map/ppermute | solution.py:43
  124.7 9.7 %collective-permute-start.12 = (bf16[1280,128]{1,0:T(8,128)(2,1)S(1)}, bf16[1280,128]{1,0:T(8,128)(2,1)S(1)}, u32[]{:S(2)}, u32[]{:S(2)}) collective-permute-start(bf16[1280,128]{1,0:T(8,128)(2,1)S(1)} %get-tuple-element.22), channel_id=1, source_target_pairs={{0,2},{1,3},{2,0},{3,1},{4,6},{5,7},{6,4},{7,5},{8,10},{9,11},{10,... | collective-permute-start | bytes 983048 | tf_op jit(solution)/shard_map/ppermute | solution.py:43
  125.3 17.7 %collective-permute-start.13 = (bf16[1280,128]{1,0:T(8,128)(2,1)S(1)}, bf16[1280,128]{1,0:T(8,128)(2,1)S(1)}, u32[]{:S(2)}, u32[]{:S(2)}) collective-permute-start(bf16[1280,128]{1,0:T(8,128)(2,1)S(1)} %get-tuple-element.23), channel_id=1, source_target_pairs={{0,1},{1,2},{2,3},{3,0},{4,5},{5,6},{6,7},{7,4},{8,9},{9,10},{10,1... | collective-permute-start | bytes 983048 | tf_op jit(solution)/shard_map/ppermute | solution.py:43
  143.3 17.2 %collective-permute-start.14 = (bf16[1280,128]{1,0:T(8,128)(2,1)S(1)}, bf16[1280,128]{1,0:T(8,128)(2,1)S(1)}, u32[]{:S(2)}, u32[]{:S(2)}) collective-permute-start(bf16[1280,128]{1,0:T(8,128)(2,1)S(1)} %multiply_convert_fusion.refs_0_), channel_id=1, source_target_pairs={{0,1},{1,2},{2,3},{3,0},{4,5},{5,6},{6,7},{7,4},{8,9},{9,10},{10,1... | collective-permute-start | bytes 983048 | tf_op jit(solution)/shard_map/ppermute | solution.py:43
  143.4 17.1 %collective-permute-start.15 = (bf16[1280,128]{1,0:T(8,128)(2,1)S(1)}, bf16[1280,128]{1,0:T(8,128)(2,1)S(1)}, u32[]{:S(2)}, u32[]{:S(2)}) collective-permute-start(bf16[1280,128]{1,0:T(8,128)(2,1)S(1)} %multiply_convert_fusion.refs_0_), channel_id=1, source_target_pairs={{0,2},{1,3},{2,0},{3,1},{4,6},{5,7},{6,4},{7,5},{8,10},{9,11},{10,... | collective-permute-start | bytes 983048 | tf_op jit(solution)/shard_map/ppermute | solution.py:43
  144.0 16.9 %collective-permute-start.16 = (bf16[1280,128]{1,0:T(8,128)(2,1)S(1)}, bf16[1280,128]{1,0:T(8,128)(2,1)S(1)}, u32[]{:S(2)}, u32[]{:S(2)}) collective-permute-start(bf16[1280,128]{1,0:T(8,128)(2,1)S(1)} %multiply_convert_fusion.refs_0_), channel_id=1, source_target_pairs={{0,3},{1,0},{2,1},{3,2},{4,7},{5,4},{6,5},{7,6},{8,11},{9,8},{10,9... | collective-permute-start | bytes 983048 | tf_op jit(solution)/shard_map/ppermute | solution.py:43
  170.6 140.0 %all-to-all-start.1 = ((bf16[32,3,224,128]{3,2,1,0:T(8,128)(2,1)}), bf16[32,3,224,128]{3,2,1,0:T(8,128)(2,1)}, u32[]{:S(2)}, u32[]{:S(2)}) async-start(bf16[32,3,224,128]{3,2,1,0:T(8,128)(2,1)} %after.4), calls=%async_computation.1 | async-start | bytes 11010048 | tf_op jit(solution)/shard_map/all_to_all | solution.py:95
  181.3 31.9 %collective-permute-start.17 = (bf16[2,160,896]{2,1,0:T(8,128)(2,1)}, bf16[2,160,896]{2,1,0:T(8,128)(2,1)S(1)}, u32[]{:S(2)}, u32[]{:S(2)}) collective-permute-start(bf16[2,160,896]{2,1,0:T(8,128)(2,1)} %get-tuple-element.25), channel_id=1, source_target_pairs={{0,192},{1,193},{2,194},{3,195},{4,196},{5,197},{6,198},{7,199},{8... | collective-permute-start | bytes 1720328 | tf_op jit(solution)/shard_map/ppermute | solution.py:43
  184.1 36.1 %collective-permute-start.18 = (bf16[2,160,896]{2,1,0:T(8,128)(2,1)S(1)}, bf16[2,160,896]{2,1,0:T(8,128)(2,1)S(1)}, u32[]{:S(2)}, u32[]{:S(2)}) collective-permute-start(bf16[2,160,896]{2,1,0:T(8,128)(2,1)S(1)} %get-tuple-element.26), channel_id=1, source_target_pairs={{0,128},{1,129},{2,130},{3,131},{4,132},{5,133},{6,134},{7,135},{8... | collective-permute-start | bytes 1720328 | tf_op jit(solution)/shard_map/ppermute | solution.py:43
  184.6 55.9 %collective-permute-start.19 = (bf16[2,160,896]{2,1,0:T(8,128)(2,1)S(1)}, bf16[2,160,896]{2,1,0:T(8,128)(2,1)S(1)}, u32[]{:S(2)}, u32[]{:S(2)}) collective-permute-start(bf16[2,160,896]{2,1,0:T(8,128)(2,1)S(1)} %get-tuple-element.27), channel_id=1, source_target_pairs={{0,64},{1,65},{2,66},{3,67},{4,68},{5,69},{6,70},{7,71},{8,72},{9,... | collective-permute-start | bytes 1720328 | tf_op jit(solution)/shard_map/ppermute | solution.py:43
  241.7 3.5 %collective-permute-start.20 = (bf16[4,160,896]{2,1,0:T(8,128)(2,1)}, bf16[4,160,896]{2,1,0:T(8,128)(2,1)S(1)}, u32[]{:S(2)}, u32[]{:S(2)}) collective-permute-start(bf16[4,160,896]{2,1,0:T(8,128)(2,1)} %pad_maximum_fusion.1), channel_id=1, source_target_pairs={{0,8},{1,9},{2,10},{3,11},{4,12},{5,13},{6,14},{7,15},{8,0},{9,1},... | collective-permute-start | bytes 3440648 | tf_op jit(solution)/shard_map/ppermute | solution.py:43
  252.3 53.6 %collective-permute-start.21 = (bf16[128,448]{1,0:T(8,128)(2,1)S(1)}, bf16[128,448]{1,0:T(8,128)(2,1)S(1)}, u32[]{:S(2)}, u32[]{:S(2)}) collective-permute-start(bf16[128,448]{1,0:T(8,128)(2,1)S(1)} %bitcast.133), channel_id=1, source_target_pairs={{0,4},{1,5},{2,6},{3,7},{4,0},{5,1},{6,2},{7,3},{8,12},{9,13},{10,... | collective-permute-start | bytes 344072 | tf_op jit(solution)/shard_map/ppermute | solution.py:43
  265.2 40.8 %collective-permute-start.22 = (bf16[128,448]{1,0:T(8,128)(2,1)S(1)}, bf16[128,448]{1,0:T(8,128)(2,1)S(1)}, u32[]{:S(2)}, u32[]{:S(2)}) collective-permute-start(bf16[128,448]{1,0:T(8,128)(2,1)S(1)} %bitcast.132), channel_id=1, source_target_pairs={{0,48},{1,49},{2,50},{3,51},{4,52},{5,53},{6,54},{7,55},{8,56},{9,... | collective-permute-start | bytes 344072 | tf_op jit(solution)/shard_map/ppermute | solution.py:43
  268.9 46.9 %collective-permute-start.23 = (bf16[128,448]{1,0:T(8,128)(2,1)S(1)}, bf16[128,448]{1,0:T(8,128)(2,1)S(1)}, u32[]{:S(2)}, u32[]{:S(2)}) collective-permute-start(bf16[128,448]{1,0:T(8,128)(2,1)S(1)} %bitcast.127), channel_id=1, source_target_pairs={{0,52},{1,53},{2,54},{3,55},{4,48},{5,49},{6,50},{7,51},{8,60},{9,... | collective-permute-start | bytes 344072 | tf_op jit(solution)/shard_map/ppermute | solution.py:43
  271.8 44.0 %collective-permute-start.24 = (bf16[128,448]{1,0:T(8,128)(2,1)S(1)}, bf16[128,448]{1,0:T(8,128)(2,1)S(1)}, u32[]{:S(2)}, u32[]{:S(2)}) collective-permute-start(bf16[128,448]{1,0:T(8,128)(2,1)S(1)} %bitcast.128), channel_id=1, source_target_pairs={{0,32},{1,33},{2,34},{3,35},{4,36},{5,37},{6,38},{7,39},{8,40},{9,... | collective-permute-start | bytes 344072 | tf_op jit(solution)/shard_map/ppermute | solution.py:43
  272.8 43.0 %collective-permute-start.25 = (bf16[128,448]{1,0:T(8,128)(2,1)S(1)}, bf16[128,448]{1,0:T(8,128)(2,1)S(1)}, u32[]{:S(2)}, u32[]{:S(2)}) collective-permute-start(bf16[128,448]{1,0:T(8,128)(2,1)S(1)} %bitcast.129), channel_id=1, source_target_pairs={{0,36},{1,37},{2,38},{3,39},{4,32},{5,33},{6,34},{7,35},{8,44},{9,... | collective-permute-start | bytes 344072 | tf_op jit(solution)/shard_map/ppermute | solution.py:43
  305.9 9.8 %collective-permute-start.26 = (bf16[128,448]{1,0:T(8,128)(2,1)S(1)}, bf16[128,448]{1,0:T(8,128)(2,1)S(1)}, u32[]{:S(2)}, u32[]{:S(2)}) collective-permute-start(bf16[128,448]{1,0:T(8,128)(2,1)S(1)} %bitcast.131), channel_id=1, source_target_pairs={{0,16},{1,17},{2,18},{3,19},{4,20},{5,21},{6,22},{7,23},{8,24},{9,... | collective-permute-start | bytes 344072 | tf_op jit(solution)/shard_map/ppermute | solution.py:43
  305.9 14.3 %collective-permute-start.27 = (bf16[128,448]{1,0:T(8,128)(2,1)S(1)}, bf16[128,448]{1,0:T(8,128)(2,1)S(1)}, u32[]{:S(2)}, u32[]{:S(2)}) collective-permute-start(bf16[128,448]{1,0:T(8,128)(2,1)S(1)} %bitcast.130), channel_id=1, source_target_pairs={{0,20},{1,21},{2,22},{3,23},{4,16},{5,17},{6,18},{7,19},{8,28},{9,... | collective-permute-start | bytes 344072 | tf_op jit(solution)/shard_map/ppermute | solution.py:43
  (5 other events, 43.4 us)

commit v3 on v2

--- a/solution.py
+++ b/solution.py
@@ -196,24 +196,31 @@
 
 
 def combine_kernel(slot, high, low, *refs):
-    outputs, out = rows_of(refs), refs[-1]
-    total = jnp.zeros(out.shape, jnp.float32)
+    outputs, outs = rows_of(refs), refs[Y + 1 :]
+    features, tokens = outs[0].shape
+    total = jnp.zeros((PAIR * features, slot.shape[1]), jnp.float32)
     for place, part in enumerate(outputs):
         rows = lax.broadcasted_iota(jnp.int32, (part.shape[0], slot.shape[1]), 0)
         found = slot[place : place + 1, :] == rows
         for gate in (high, low):
             share = jnp.where(found, gate[place : place + 1, :], 0.0).astype(jnp.bfloat16)
             total += lax.dot_general(
-                share, part[...], (((0,), (0,)), ((), ())), preferred_element_type=jnp.float32
+                part[...], share, (((0,), (0,)), ((), ())), preferred_element_type=jnp.float32
             )
-    out[...] = total
+    for number, out in enumerate(outs):
+        source, half = number // PAIR, number % PAIR
+        out[...] = total[
+            half * features : (half + 1) * features, source * tokens : (source + 1) * tokens
+        ].astype(jnp.bfloat16)
 
 
 def combine(slot, high, low, outputs):
     tokens, features = slot.shape[1], outputs[0].shape[2]
     flops = 4 * slot.size * outputs[0].shape[1] * features
-    shape = jax.ShapeDtypeStruct((tokens, features), jnp.float32)
-    return whole(combine_kernel, [slot, high, low, *outputs], [shape], flops, "combine")[0]
+    shape = jax.ShapeDtypeStruct((features // PAIR, tokens // Z), jnp.bfloat16)
+    return whole(
+        combine_kernel, [slot, high, low, *outputs], [shape] * (Z * PAIR), flops, "combine"
+    )
 
 
 def local(tokens, routing, gate_weights, owner, weights, grads, first, second):
@@ -288,23 +295,23 @@
     hidden = jax.nn.silu(total).astype(jnp.bfloat16)
 
     every = [shift(hidden, dx=dx) for dx in range(X)]
+
+    holder = jnp.sum(order[None, :] * (owner[None, :] == order[:, None]), axis=1)
+    holder = after(holder, hidden)
+    arrived = exchange(jnp.take(spread, holder, axis=0, mode="clip"))
+
     expert_out = down_project(every, [block[1] for block in blocks])
 
-    holder = jnp.sum(order[None, :] * (owner[None, :] == order[:, None]), axis=1)
-    arrived = exchange(after(jnp.take(spread, holder, axis=0, mode="clip"), expert_out[0]))
-
     returned = plane_shift(expert_out, -1)
 
     partial = combine(slot, high, low, returned)
-    partial = partial.astype(jnp.bfloat16).reshape(Z, token_count, PAIR, features)
     moved = [arrived[:, place].reshape(state_shape) for place in range(3)]
     mixed = sum(
-        shift(partial[dz, :, dpair], dz=-dz, dpair=dpair).astype(jnp.float32)
-        for dz in range(Z)
-        for dpair in range(PAIR)
-        if dz or dpair
-    )
-    mixed += after(partial[0, :, 0], *moved).astype(jnp.float32)
+        shift(part, dz=-(number // PAIR), dpair=number % PAIR).astype(jnp.float32)
+        for number, part in enumerate(partial)
+        if number
+    )
+    mixed = (mixed + after(partial[0], *moved).astype(jnp.float32)).T
     return (mixed.astype(jnp.bfloat16), *moved)
 
 

time: 325 us -> 319 us (0.982)
  waiting for transfers between devices: 185 us -> 177 us
  starting transfers between devices: 83.5 us -> 88.6 us
  local copies, waits for them, and re-layouts: 25.8 us -> 21.6 us
    all_to_all x2, starting transfers between devices: 18.2 us -> 28.4 us  [exchange(): lax.all_to_all(array, 'expert', split_axis=0, concat_axis=0, tiled=True)]
    ppermute x28, waiting for transfers between devices: 185 us -> 177 us  [shift(): return lax.ppermute(array, ('expert', 'cuts'), pairs)]
    ppermute x28, starting transfers between devices: 65.3 us -> 60.3 us  [shift(): return lax.ppermute(array, ('expert', 'cuts'), pairs)]
  transfers between devices with their start and end apart: 30 -> 30, of which waited for: 15 -> 15; matrix products, arithmetic and copies ran while one was open for 7% -> 7% of each run, Pallas kernels for 6% -> 7%
where the time goes in v3:
time: 319 us; the launch traced here: 318 us
  waiting for transfers between devices  177 us (55%)
  starting transfers between devices  88.6 us (28%)
  local copies, waits for them, and re-layouts  21.6 us (7%)
  Pallas kernels  20.9 us (7%)
  other arithmetic  9.15 us (3%)
    ppermute x28, waiting for transfers between devices, shift(): return lax.ppermute(array, ('expert', 'cuts'), pairs)  177 us
    ppermute x28, starting transfers between devices, shift(): return lax.ppermute(array, ('expert', 'cuts'), pairs)  60.3 us
    all_to_all x2, starting transfers between devices, exchange(): lax.all_to_all(array, 'expert', split_axis=0, concat_axis=0, tiled=True)  28.4 us
    pallas_call x4, Pallas kernels, whole(): pl.pallas_call(kernel, in_specs=[vmem] * len(inputs), out_specs=[vmem] *...  11.6 us
    pallas_call x1, Pallas kernels, adamw(): pl.pallas_call(adamw_kernel, grid=(steps,), in_specs=[block] * 4, out_spe...  9.28 us
  transfers between devices with their start and end apart: 30, of which 15 were waited for; matrix products, arithmetic and copies ran while one was open for 7% of the time, Pallas kernels for 7%

profile of v3, /device:TPU:1, one launch (start us, length us, event | category | flops | bytes accessed | tf_op | source)
XLA Modules:
  0.0 318.1 jit_solution(6169310143269443347)
XLA Ops:
  1.6 2.6 collective-permute-start
  6.7 3.8 %collective-permute-start.1 = (bf16[128,960]{1,0:T(8,128)(2,1)S(1)}, bf16[128,960]{1,0:T(8,128)(2,1)S(1)}, u32[]{:S(2)}, u32[]{:S(2)}) collective-permute-start(bf16[128,960]{1,0:T(8,128)(2,1)S(1)} %pad_maximum_fusion.12), channel_id=1, source_target_pairs={{0,16},{1,17},{2,18},{3,19},{4,20},{5,21},{6,22},{7,23},{8,24},{9,... | collective-permute-start | bytes 737288 | tf_op jit(solution)/shard_map/ppermute | solution.py:43
  10.5 4.7 %collective-permute-start.2 = (bf16[128,960]{1,0:T(8,128)(2,1)S(1)}, bf16[128,960]{1,0:T(8,128)(2,1)S(1)}, u32[]{:S(2)}, u32[]{:S(2)}) collective-permute-start(bf16[128,960]{1,0:T(8,128)(2,1)S(1)} %pad_maximum_fusion.12), channel_id=1, source_target_pairs={{0,32},{1,33},{2,34},{3,35},{4,36},{5,37},{6,38},{7,39},{8,40},{9,... | collective-permute-start | bytes 737288 | tf_op jit(solution)/shard_map/ppermute | solution.py:43
  15.2 2.4 collective-permute-start.3
  17.6 9.3 %adamw.1 = bf16[32,3,224,128]{3,2,1,0:T(8,128)(2,1)} custom-call(bf16[32,224,128]{2,1,0:T(8,128)(2,1)} %bitcast.100, bf16[32,224,128]{2,1,0:T(8,128)(2,1)} %bitcast.101, bf16[32,224,128]{2,1,0:T(8,128)(2,1)} %bitcast.102, bf16[32,224,128]{2,1,0:T(8,128)(2,1)} %bitcast.103), custom_call_target="tpu_custom_call" | custom-call | flops 11010048 | bytes 12845056 | tf_op jit(solution)/shard_map/adamw/pallas_call | solution.py:64
  26.9 7.5 %all-to-all-start = ((bf16[32,3,224,128]{3,2,1,0:T(8,128)(2,1)}), bf16[32,3,224,128]{3,2,1,0:T(8,128)(2,1)}, u32[]{:S(2)}, u32[]{:S(2)}) async-start(bf16[32,3,224,128]{3,2,1,0:T(8,128)(2,1)} %adamw.1), calls=%async_computation | async-start | bytes 11010048 | tf_op jit(solution)/shard_map/all_to_all | solution.py:95
  34.6 4.6 %collective-permute-done.3 = bf16[128,960]{1,0:T(8,128)(2,1)S(1)} collective-permute-done((bf16[128,960]{1,0:T(8,128)(2,1)S(1)}, bf16[128,960]{1,0:T(8,128)(2,1)S(1)}, u32[]{:S(2)}, u32[]{:S(2)}) %collective-permute-start.3) | collective-permute-done | bytes 245792 | tf_op jit(solution)/shard_map/ppermute | solution.py:43
  43.4 2.8 slice.95
  48.0 2.8 collective-permute-start.5
  51.8 2.6 collective-permute-start.9
  55.0 41.3 %collective-permute-done.4.refs_1_ = bf16[2,160,896]{2,1,0:T(8,128)(2,1)S(1)} collective-permute-done((bf16[2,160,896]{2,1,0:T(8,128)(2,1)}, bf16[2,160,896]{2,1,0:T(8,128)(2,1)S(1)}, u32[]{:S(2)}, u32[]{:S(2)}) %collective-permute-start.4) | collective-permute-done | bytes 573472 | tf_op jit(solution)/shard_map/ppermute | solution.py:43
  98.4 16.4 %collective-permute-done.5.refs_2_ = bf16[2,160,896]{2,1,0:T(8,128)(2,1)S(1)} collective-permute-done((bf16[2,160,896]{2,1,0:T(8,128)(2,1)}, bf16[2,160,896]{2,1,0:T(8,128)(2,1)S(1)}, u32[]{:S(2)}, u32[]{:S(2)}) %collective-permute-start.5) | collective-permute-done | bytes 573472 | tf_op jit(solution)/shard_map/ppermute | solution.py:43
  122.5 2.6 collective-permute-start.11
  126.8 12.2 %collective-permute-done.11 = bf16[1280,128]{1,0:T(8,128)(2,1)S(1)} collective-permute-done((bf16[1280,128]{1,0:T(8,128)(2,1)S(1)}, bf16[1280,128]{1,0:T(8,128)(2,1)S(1)}, u32[]{:S(2)}, u32[]{:S(2)}) %collective-permute-start.11) | collective-permute-done | bytes 327712 | tf_op jit(solution)/shard_map/ppermute | solution.py:43
  139.1 4.3 %collective-permute-done.13 = bf16[1280,128]{1,0:T(8,128)(2,1)S(1)} collective-permute-done((bf16[1280,128]{1,0:T(8,128)(2,1)S(1)}, bf16[1280,128]{1,0:T(8,128)(2,1)S(1)}, u32[]{:S(2)}, u32[]{:S(2)}) %collective-permute-start.13) | collective-permute-done | bytes 327712 | tf_op jit(solution)/shard_map/ppermute | solution.py:43
  145.0 6.3 %gather_fusion = bf16[32,3,224,128]{3,2,1,0:T(8,128)(2,1)} fusion(bf16[32,3,224,128]{3,2,1,0:T(8,128)(2,1)} %all-to-all-done, s32[1024]{0:T(1024)S(1)} %pad_clamp_fusion), kind=kCustom, calls=%fused_computation | custom fusion | bytes 11010176 | tf_op jit(solution)/shard_map/jit(_take)/gather | solution.py:301
  151.3 20.9 %all-to-all-start.1 = ((bf16[32,3,224,128]{3,2,1,0:T(8,128)(2,1)}), bf16[32,3,224,128]{3,2,1,0:T(8,128)(2,1)}, u32[]{:S(2)}, u32[]{:S(2)}) async-start(bf16[32,3,224,128]{3,2,1,0:T(8,128)(2,1)} %gather_fusion), calls=%async_computation.1 | async-start | bytes 11010048 | tf_op jit(solution)/shard_map/all_to_all | solution.py:95
  173.5 2.5 collective-permute-start.15
  177.1 5.5 %collective-permute-done.14.refs_1_ = bf16[1280,128]{1,0:T(8,128)(2,1)S(1)} collective-permute-done((bf16[1280,128]{1,0:T(8,128)(2,1)S(1)}, bf16[1280,128]{1,0:T(8,128)(2,1)S(1)}, u32[]{:S(2)}, u32[]{:S(2)}) %collective-permute-start.14) | collective-permute-done | bytes 327712 | tf_op jit(solution)/shard_map/ppermute | solution.py:43
  182.6 8.0 %collective-permute-done.15.refs_2_ = bf16[1280,128]{1,0:T(8,128)(2,1)S(1)} collective-permute-done((bf16[1280,128]{1,0:T(8,128)(2,1)S(1)}, bf16[1280,128]{1,0:T(8,128)(2,1)S(1)}, u32[]{:S(2)}, u32[]{:S(2)}) %collective-permute-start.15) | collective-permute-done | bytes 327712 | tf_op jit(solution)/shard_map/ppermute | solution.py:43
  193.0 2.6 collective-permute-start.17
  196.7 36.4 %collective-permute-done.17.refs_1_ = bf16[2,160,896]{2,1,0:T(8,128)(2,1)S(1)} collective-permute-done((bf16[2,160,896]{2,1,0:T(8,128)(2,1)S(1)}, bf16[2,160,896]{2,1,0:T(8,128)(2,1)S(1)}, u32[]{:S(2)}, u32[]{:S(2)}) %collective-permute-start.17) | collective-permute-done | bytes 573472 | tf_op jit(solution)/shard_map/ppermute | solution.py:43
  234.9 16.9 %collective-permute-done.19.refs_3_ = bf16[2,160,896]{2,1,0:T(8,128)(2,1)S(1)} collective-permute-done((bf16[2,160,896]{2,1,0:T(8,128)(2,1)S(1)}, bf16[2,160,896]{2,1,0:T(8,128)(2,1)S(1)}, u32[]{:S(2)}, u32[]{:S(2)}) %collective-permute-start.19) | collective-permute-done | bytes 573472 | tf_op jit(solution)/shard_map/ppermute | solution.py:43
  253.9 2.7 collective-permute-done.20.refs_4_
  256.7 5.3 %combine.1 = (bf16[448,128]{1,0:T(8,128)(2,1)S(1)}, bf16[448,128]{1,0:T(8,128)(2,1)S(1)}, bf16[448,128]{1,0:T(8,128)(2,1)S(1)}, bf16[448,128]{1,0:T(8,128)(2,1)S...) custom-call(s32[8,512]{1,0:T(8,128)S(1)} %reshape.85.slot, ...), custom_call_target="tpu_custom_call" | custom-call | flops 2348810240 | bytes 4407296 | tf_op jit(solution)/shard_map/combine/pallas_call | solution.py:101
  264.7 7.2 %collective-permute-start.23 = (bf16[448,128]{1,0:T(8,128)(2,1)S(1)}, bf16[448,128]{1,0:T(8,128)(2,1)S(1)}, u32[]{:S(2)}, u32[]{:S(2)}) collective-permute-start(bf16[448,128]{1,0:T(8,128)(2,1)S(1)} %get-tuple-element.38), channel_id=1, source_target_pairs={{0,52},{1,53},{2,54},{3,55},{4,48},{5,49},{6,50},{7,51},{8,60},{9,... | collective-permute-start | bytes 344072 | tf_op jit(solution)/shard_map/ppermute | solution.py:43
  272.0 5.1 %collective-permute-start.25 = (bf16[448,128]{1,0:T(8,128)(2,1)S(1)}, bf16[448,128]{1,0:T(8,128)(2,1)S(1)}, u32[]{:S(2)}, u32[]{:S(2)}) collective-permute-start(bf16[448,128]{1,0:T(8,128)(2,1)S(1)} %get-tuple-element.40), channel_id=1, source_target_pairs={{0,36},{1,37},{2,38},{3,39},{4,32},{5,33},{6,34},{7,35},{8,44},{9,... | collective-permute-start | bytes 344072 | tf_op jit(solution)/shard_map/ppermute | solution.py:43
  277.1 19.0 %collective-permute-done.21 = bf16[448,128]{1,0:T(8,128)(2,1)S(1)} collective-permute-done((bf16[448,128]{1,0:T(8,128)(2,1)S(1)}, bf16[448,128]{1,0:T(8,128)(2,1)S(1)}, u32[]{:S(2)}, u32[]{:S(2)}) %collective-permute-start.21) | collective-permute-done | bytes 114720 | tf_op jit(solution)/shard_map/ppermute | solution.py:43
  296.0 5.4 %collective-permute-start.26 = (bf16[448,128]{1,0:T(8,128)(2,1)S(1)}, bf16[448,128]{1,0:T(8,128)(2,1)S(1)}, u32[]{:S(2)}, u32[]{:S(2)}) collective-permute-start(bf16[448,128]{1,0:T(8,128)(2,1)S(1)} %get-tuple-element.41), channel_id=1, source_target_pairs={{0,16},{1,17},{2,18},{3,19},{4,20},{5,21},{6,22},{7,23},{8,24},{9,... | collective-permute-start | bytes 344072 | tf_op jit(solution)/shard_map/ppermute | solution.py:43
  301.4 2.9 collective-permute-start.27
  304.3 5.2 %fusion.25 = (bf16[32,1,224,128]{3,2,1,0:T(8,128)(2,1)}, bf16[32,1,224,128]{3,2,1,0:T(8,128)(2,1)}, bf16[32,1,224,128]{3,2,1,0:T(8,128)(2,1)}) fusion(bf16[32,3,224,128]{3,2,1,0:T(8,128)(2,1)} %all-to-all-done.1), kind=kLoop, calls=%fused_computation.87 | loop fusion | bytes 11010048 | tf_op jit(solution)/shard_map/slice | solution.py:308
  309.6 6.8 %collective-permute-done.27 = bf16[448,128]{1,0:T(8,128)(2,1)S(1)} collective-permute-done((bf16[448,128]{1,0:T(8,128)(2,1)S(1)}, bf16[448,128]{1,0:T(8,128)(2,1)S(1)}, u32[]{:S(2)}, u32[]{:S(2)}) %collective-permute-start.27) | collective-permute-done | bytes 114720 | tf_op jit(solution)/shard_map/ppermute | solution.py:43
  (88 shorter events, 38.5 us)
Async XLA Ops:
  1.6 4.9 %collective-permute-start = (bf16[128,448]{1,0:T(8,128)(2,1)S(1)}, bf16[128,448]{1,0:T(8,128)(2,1)S(1)}, u32[]{:S(2)}, u32[]{:S(2)}) collective-permute-start(bf16[128,448]{1,0:T(8,128)(2,1)S(1)} %copy.56), channel_id=1, source_target_pairs={{0,4},{1,5},{2,6},{3,7},{4,0},{5,1},{6,2},{7,3},{8,12},{9,13},{10,... | collective-permute-start | bytes 344072 | tf_op jit(solution)/shard_map/ppermute | solution.py:43
  6.7 27.9 %collective-permute-start.1 = (bf16[128,960]{1,0:T(8,128)(2,1)S(1)}, bf16[128,960]{1,0:T(8,128)(2,1)S(1)}, u32[]{:S(2)}, u32[]{:S(2)}) collective-permute-start(bf16[128,960]{1,0:T(8,128)(2,1)S(1)} %pad_maximum_fusion.12), channel_id=1, source_target_pairs={{0,16},{1,17},{2,18},{3,19},{4,20},{5,21},{6,22},{7,23},{8,24},{9,... | collective-permute-start | bytes 737288 | tf_op jit(solution)/shard_map/ppermute | solution.py:43
  10.5 24.1 %collective-permute-start.2 = (bf16[128,960]{1,0:T(8,128)(2,1)S(1)}, bf16[128,960]{1,0:T(8,128)(2,1)S(1)}, u32[]{:S(2)}, u32[]{:S(2)}) collective-permute-start(bf16[128,960]{1,0:T(8,128)(2,1)S(1)} %pad_maximum_fusion.12), channel_id=1, source_target_pairs={{0,32},{1,33},{2,34},{3,35},{4,36},{5,37},{6,38},{7,39},{8,40},{9,... | collective-permute-start | bytes 737288 | tf_op jit(solution)/shard_map/ppermute | solution.py:43
  15.2 23.9 %collective-permute-start.3 = (bf16[128,960]{1,0:T(8,128)(2,1)S(1)}, bf16[128,960]{1,0:T(8,128)(2,1)S(1)}, u32[]{:S(2)}, u32[]{:S(2)}) collective-permute-start(bf16[128,960]{1,0:T(8,128)(2,1)S(1)} %pad_maximum_fusion.12), channel_id=1, source_target_pairs={{0,48},{1,49},{2,50},{3,51},{4,52},{5,53},{6,54},{7,55},{8,56},{9,... | collective-permute-start | bytes 737288 | tf_op jit(solution)/shard_map/ppermute | solution.py:43
  26.9 118.1 %all-to-all-start = ((bf16[32,3,224,128]{3,2,1,0:T(8,128)(2,1)}), bf16[32,3,224,128]{3,2,1,0:T(8,128)(2,1)}, u32[]{:S(2)}, u32[]{:S(2)}) async-start(bf16[32,3,224,128]{3,2,1,0:T(8,128)(2,1)} %adamw.1), calls=%async_computation | async-start | bytes 11010048 | tf_op jit(solution)/shard_map/all_to_all | solution.py:95
  42.2 54.1 %collective-permute-start.4 = (bf16[2,160,896]{2,1,0:T(8,128)(2,1)}, bf16[2,160,896]{2,1,0:T(8,128)(2,1)S(1)}, u32[]{:S(2)}, u32[]{:S(2)}) collective-permute-start(bf16[2,160,896]{2,1,0:T(8,128)(2,1)} %get-tuple-element.25), channel_id=1, source_target_pairs={{0,64},{1,65},{2,66},{3,67},{4,68},{5,69},{6,70},{7,71},{8,72},{9,... | collective-permute-start | bytes 1720328 | tf_op jit(solution)/shard_map/ppermute | solution.py:43
  48.0 66.9 %collective-permute-start.5 = (bf16[2,160,896]{2,1,0:T(8,128)(2,1)}, bf16[2,160,896]{2,1,0:T(8,128)(2,1)S(1)}, u32[]{:S(2)}, u32[]{:S(2)}) collective-permute-start(bf16[2,160,896]{2,1,0:T(8,128)(2,1)} %get-tuple-element.26), channel_id=1, source_target_pairs={{0,128},{1,129},{2,130},{3,131},{4,132},{5,133},{6,134},{7,135},{8... | collective-permute-start | bytes 1720328 | tf_op jit(solution)/shard_map/ppermute | solution.py:43
  50.8 64.1 %collective-permute-start.6 = (bf16[2,160,896]{2,1,0:T(8,128)(2,1)S(1)}, bf16[2,160,896]{2,1,0:T(8,128)(2,1)S(1)}, u32[]{:S(2)}, u32[]{:S(2)}) collective-permute-start(bf16[2,160,896]{2,1,0:T(8,128)(2,1)S(1)} %get-tuple-element.27), channel_id=1, source_target_pairs={{0,192},{1,193},{2,194},{3,195},{4,196},{5,197},{6,198},{7,199},{8... | collective-permute-start | bytes 1720328 | tf_op jit(solution)/shard_map/ppermute | solution.py:43
  51.8 64.3 %collective-permute-start.9 = (bf16[2,896,128]{2,1,0:T(8,128)(2,1)S(1)}, bf16[2,896,128]{2,1,0:T(8,128)(2,1)}, u32[]{:S(2)}, u32[]{:S(2)}) collective-permute-start(bf16[2,896,128]{2,1,0:T(8,128)(2,1)S(1)} %pad_maximum_fusion.11), channel_id=1, source_target_pairs={{0,3},{1,0},{2,1},{3,2},{4,7},{5,4},{6,5},{7,6},{8,11},{9,8},{10,9... | collective-permute-start | bytes 1376264 | tf_op jit(solution)/shard_map/ppermute | solution.py:43
  54.4 61.7 %collective-permute-start.8 = (bf16[2,896,128]{2,1,0:T(8,128)(2,1)S(1)}, bf16[2,896,128]{2,1,0:T(8,128)(2,1)}, u32[]{:S(2)}, u32[]{:S(2)}) collective-permute-start(bf16[2,896,128]{2,1,0:T(8,128)(2,1)S(1)} %pad_maximum_fusion.10), channel_id=1, source_target_pairs={{0,2},{1,3},{2,0},{3,1},{4,6},{5,7},{6,4},{7,5},{8,10},{9,11},{10,... | collective-permute-start | bytes 1376264 | tf_op jit(solution)/shard_map/ppermute | solution.py:43
  96.3 19.7 %collective-permute-start.7 = (bf16[2,896,128]{2,1,0:T(8,128)(2,1)S(1)}, bf16[2,896,128]{2,1,0:T(8,128)(2,1)}, u32[]{:S(2)}, u32[]{:S(2)}) collective-permute-start(bf16[2,896,128]{2,1,0:T(8,128)(2,1)S(1)} %pad_maximum_fusion.9), channel_id=1, source_target_pairs={{0,1},{1,2},{2,3},{3,0},{4,5},{5,6},{6,7},{7,4},{8,9},{9,10},{10,1... | collective-permute-start | bytes 1376264 | tf_op jit(solution)/shard_map/ppermute | solution.py:43
  116.1 4.7 %collective-permute-start.10 = (bf16[4,160,896]{2,1,0:T(8,128)(2,1)}, bf16[4,160,896]{2,1,0:T(8,128)(2,1)S(1)}, u32[]{:S(2)}, u32[]{:S(2)}) collective-permute-start(bf16[4,160,896]{2,1,0:T(8,128)(2,1)} %after.3), channel_id=1, source_target_pairs={{0,8},{1,9},{2,10},{3,11},{4,12},{5,13},{6,14},{7,15},{8,0},{9,1},... | collective-permute-start | bytes 3440648 | tf_op jit(solution)/shard_map/ppermute | solution.py:43
  120.9 5.3 %copy-start.2 = (s32[32]{0:T(128)S(1)}, s32[32]{0:T(128)}, u32[]{:S(2)}) copy-start(s32[32]{0:T(128)} %param.11) | copy-start | bytes 388
  122.5 16.6 %collective-permute-start.11 = (bf16[1280,128]{1,0:T(8,128)(2,1)S(1)}, bf16[1280,128]{1,0:T(8,128)(2,1)S(1)}, u32[]{:S(2)}, u32[]{:S(2)}) collective-permute-start(bf16[1280,128]{1,0:T(8,128)(2,1)S(1)} %get-tuple-element.29), channel_id=1, source_target_pairs={{0,3},{1,0},{2,1},{3,2},{4,7},{5,4},{6,5},{7,6},{8,11},{9,8},{10,9... | collective-permute-start | bytes 983048 | tf_op jit(solution)/shard_map/ppermute | solution.py:43
  125.1 14.0 %collective-permute-start.12 = (bf16[1280,128]{1,0:T(8,128)(2,1)S(1)}, bf16[1280,128]{1,0:T(8,128)(2,1)S(1)}, u32[]{:S(2)}, u32[]{:S(2)}) collective-permute-start(bf16[1280,128]{1,0:T(8,128)(2,1)S(1)} %get-tuple-element.30), channel_id=1, source_target_pairs={{0,2},{1,3},{2,0},{3,1},{4,6},{5,7},{6,4},{7,5},{8,10},{9,11},{10,... | collective-permute-start | bytes 983048 | tf_op jit(solution)/shard_map/ppermute | solution.py:43
  125.6 17.7 %collective-permute-start.13 = (bf16[1280,128]{1,0:T(8,128)(2,1)S(1)}, bf16[1280,128]{1,0:T(8,128)(2,1)S(1)}, u32[]{:S(2)}, u32[]{:S(2)}) collective-permute-start(bf16[1280,128]{1,0:T(8,128)(2,1)S(1)} %get-tuple-element.31), channel_id=1, source_target_pairs={{0,1},{1,2},{2,3},{3,0},{4,5},{5,6},{6,7},{7,4},{8,9},{9,10},{10,1... | collective-permute-start | bytes 983048 | tf_op jit(solution)/shard_map/ppermute | solution.py:43
  151.3 20.9 %copy-start = (bf16[1280,128]{1,0:T(8,128)(2,1)S(1)}, bf16[1280,128]{1,0:T(8,128)(2,1)}, u32[]{:S(2)}) copy-start(bf16[1280,128]{1,0:T(8,128)(2,1)} %multiply_convert_fusion.refs_0_) | copy-start | bytes 983044
  151.3 153.0 %all-to-all-start.1 = ((bf16[32,3,224,128]{3,2,1,0:T(8,128)(2,1)}), bf16[32,3,224,128]{3,2,1,0:T(8,128)(2,1)}, u32[]{:S(2)}, u32[]{:S(2)}) async-start(bf16[32,3,224,128]{3,2,1,0:T(8,128)(2,1)} %gather_fusion), calls=%async_computation.1 | async-start | bytes 11010048 | tf_op jit(solution)/shard_map/all_to_all | solution.py:95
  172.2 10.4 %collective-permute-start.14 = (bf16[1280,128]{1,0:T(8,128)(2,1)S(1)}, bf16[1280,128]{1,0:T(8,128)(2,1)S(1)}, u32[]{:S(2)}, u32[]{:S(2)}) collective-permute-start(bf16[1280,128]{1,0:T(8,128)(2,1)S(1)} %copy-done), channel_id=1, source_target_pairs={{0,1},{1,2},{2,3},{3,0},{4,5},{5,6},{6,7},{7,4},{8,9},{9,10},{10,1... | collective-permute-start | bytes 983048 | tf_op jit(solution)/shard_map/ppermute | solution.py:43
  173.5 17.1 %collective-permute-start.15 = (bf16[1280,128]{1,0:T(8,128)(2,1)S(1)}, bf16[1280,128]{1,0:T(8,128)(2,1)S(1)}, u32[]{:S(2)}, u32[]{:S(2)}) collective-permute-start(bf16[1280,128]{1,0:T(8,128)(2,1)S(1)} %copy-done), channel_id=1, source_target_pairs={{0,2},{1,3},{2,0},{3,1},{4,6},{5,7},{6,4},{7,5},{8,10},{9,11},{10,... | collective-permute-start | bytes 983048 | tf_op jit(solution)/shard_map/ppermute | solution.py:43
  175.9 14.7 %collective-permute-start.16 = (bf16[1280,128]{1,0:T(8,128)(2,1)S(1)}, bf16[1280,128]{1,0:T(8,128)(2,1)S(1)}, u32[]{:S(2)}, u32[]{:S(2)}) collective-permute-start(bf16[1280,128]{1,0:T(8,128)(2,1)S(1)} %copy-done), channel_id=1, source_target_pairs={{0,3},{1,0},{2,1},{3,2},{4,7},{5,4},{6,5},{7,6},{8,11},{9,8},{10,9... | collective-permute-start | bytes 983048 | tf_op jit(solution)/shard_map/ppermute | solution.py:43
  193.0 40.2 %collective-permute-start.17 = (bf16[2,160,896]{2,1,0:T(8,128)(2,1)S(1)}, bf16[2,160,896]{2,1,0:T(8,128)(2,1)S(1)}, u32[]{:S(2)}, u32[]{:S(2)}) collective-permute-start(bf16[2,160,896]{2,1,0:T(8,128)(2,1)S(1)} %get-tuple-element.33), channel_id=1, source_target_pairs={{0,192},{1,193},{2,194},{3,195},{4,196},{5,197},{6,198},{7,199},{8... | collective-permute-start | bytes 1720328 | tf_op jit(solution)/shard_map/ppermute | solution.py:43
  195.6 39.3 %collective-permute-start.18 = (bf16[2,160,896]{2,1,0:T(8,128)(2,1)S(1)}, bf16[2,160,896]{2,1,0:T(8,128)(2,1)S(1)}, u32[]{:S(2)}, u32[]{:S(2)}) collective-permute-start(bf16[2,160,896]{2,1,0:T(8,128)(2,1)S(1)} %get-tuple-element.34), channel_id=1, source_target_pairs={{0,128},{1,129},{2,130},{3,131},{4,132},{5,133},{6,134},{7,135},{8... | collective-permute-start | bytes 1720328 | tf_op jit(solution)/shard_map/ppermute | solution.py:43
  196.1 55.7 %collective-permute-start.19 = (bf16[2,160,896]{2,1,0:T(8,128)(2,1)S(1)}, bf16[2,160,896]{2,1,0:T(8,128)(2,1)S(1)}, u32[]{:S(2)}, u32[]{:S(2)}) collective-permute-start(bf16[2,160,896]{2,1,0:T(8,128)(2,1)S(1)} %get-tuple-element.35), channel_id=1, source_target_pairs={{0,64},{1,65},{2,66},{3,67},{4,68},{5,69},{6,70},{7,71},{8,72},{9,... | collective-permute-start | bytes 1720328 | tf_op jit(solution)/shard_map/ppermute | solution.py:43
  253.0 3.6 %collective-permute-start.20 = (bf16[4,160,896]{2,1,0:T(8,128)(2,1)}, bf16[4,160,896]{2,1,0:T(8,128)(2,1)}, u32[]{:S(2)}, u32[]{:S(2)}) collective-permute-start(bf16[4,160,896]{2,1,0:T(8,128)(2,1)} %pad_maximum_fusion.1), channel_id=1, source_target_pairs={{0,8},{1,9},{2,10},{3,11},{4,12},{5,13},{6,14},{7,15},{8,0},{9,1},... | collective-permute-start | bytes 3440648 | tf_op jit(solution)/shard_map/ppermute | solution.py:43
  262.6 33.4 %collective-permute-start.21 = (bf16[448,128]{1,0:T(8,128)(2,1)S(1)}, bf16[448,128]{1,0:T(8,128)(2,1)S(1)}, u32[]{:S(2)}, u32[]{:S(2)}) collective-permute-start(bf16[448,128]{1,0:T(8,128)(2,1)S(1)} %get-tuple-element.36), channel_id=1, source_target_pairs={{0,4},{1,5},{2,6},{3,7},{4,0},{5,1},{6,2},{7,3},{8,12},{9,13},{10,... | collective-permute-start | bytes 344072 | tf_op jit(solution)/shard_map/ppermute | solution.py:43
  262.6 38.8 %collective-permute-start.22 = (bf16[448,128]{1,0:T(8,128)(2,1)S(1)}, bf16[448,128]{1,0:T(8,128)(2,1)S(1)}, u32[]{:S(2)}, u32[]{:S(2)}) collective-permute-start(bf16[448,128]{1,0:T(8,128)(2,1)S(1)} %get-tuple-element.37), channel_id=1, source_target_pairs={{0,48},{1,49},{2,50},{3,51},{4,52},{5,53},{6,54},{7,55},{8,56},{9,... | collective-permute-start | bytes 344072 | tf_op jit(solution)/shard_map/ppermute | solution.py:43
  264.7 44.8 %collective-permute-start.23 = (bf16[448,128]{1,0:T(8,128)(2,1)S(1)}, bf16[448,128]{1,0:T(8,128)(2,1)S(1)}, u32[]{:S(2)}, u32[]{:S(2)}) collective-permute-start(bf16[448,128]{1,0:T(8,128)(2,1)S(1)} %get-tuple-element.38), channel_id=1, source_target_pairs={{0,52},{1,53},{2,54},{3,55},{4,48},{5,49},{6,50},{7,51},{8,60},{9,... | collective-permute-start | bytes 344072 | tf_op jit(solution)/shard_map/ppermute | solution.py:43
  272.0 37.5 %collective-permute-start.24 = (bf16[448,128]{1,0:T(8,128)(2,1)S(1)}, bf16[448,128]{1,0:T(8,128)(2,1)S(1)}, u32[]{:S(2)}, u32[]{:S(2)}) collective-permute-start(bf16[448,128]{1,0:T(8,128)(2,1)S(1)} %get-tuple-element.39), channel_id=1, source_target_pairs={{0,32},{1,33},{2,34},{3,35},{4,36},{5,37},{6,38},{7,39},{8,40},{9,... | collective-permute-start | bytes 344072 | tf_op jit(solution)/shard_map/ppermute | solution.py:43
  272.0 37.7 %collective-permute-start.25 = (bf16[448,128]{1,0:T(8,128)(2,1)S(1)}, bf16[448,128]{1,0:T(8,128)(2,1)S(1)}, u32[]{:S(2)}, u32[]{:S(2)}) collective-permute-start(bf16[448,128]{1,0:T(8,128)(2,1)S(1)} %get-tuple-element.40), channel_id=1, source_target_pairs={{0,36},{1,37},{2,38},{3,39},{4,32},{5,33},{6,34},{7,35},{8,44},{9,... | collective-permute-start | bytes 344072 | tf_op jit(solution)/shard_map/ppermute | solution.py:43
  296.0 13.6 %collective-permute-start.26 = (bf16[448,128]{1,0:T(8,128)(2,1)S(1)}, bf16[448,128]{1,0:T(8,128)(2,1)S(1)}, u32[]{:S(2)}, u32[]{:S(2)}) collective-permute-start(bf16[448,128]{1,0:T(8,128)(2,1)S(1)} %get-tuple-element.41), channel_id=1, source_target_pairs={{0,16},{1,17},{2,18},{3,19},{4,20},{5,21},{6,22},{7,23},{8,24},{9,... | collective-permute-start | bytes 344072 | tf_op jit(solution)/shard_map/ppermute | solution.py:43
  301.4 15.0 %collective-permute-start.27 = (bf16[448,128]{1,0:T(8,128)(2,1)S(1)}, bf16[448,128]{1,0:T(8,128)(2,1)S(1)}, u32[]{:S(2)}, u32[]{:S(2)}) collective-permute-start(bf16[448,128]{1,0:T(8,128)(2,1)S(1)} %get-tuple-element.42), channel_id=1, source_target_pairs={{0,20},{1,21},{2,22},{3,23},{4,16},{5,17},{6,18},{7,19},{8,28},{9,... | collective-permute-start | bytes 344072 | tf_op jit(solution)/shard_map/ppermute | solution.py:43
  (1 other events, 0.6 us)

commit v4 on v3

--- a/solution.py
+++ b/solution.py
@@ -195,6 +195,9 @@
     )
 
 
+DIRECT, PAIRED = (0, 2, 3, 4, 6, 7), (1, 5)
+
+
 def combine_kernel(slot, high, low, *refs):
     outputs, outs = rows_of(refs), refs[Y + 1 :]
     features, tokens = outs[0].shape
@@ -207,20 +210,25 @@
             total += lax.dot_general(
                 part[...], share, (((0,), (0,)), ((), ())), preferred_element_type=jnp.float32
             )
-    for number, out in enumerate(outs):
-        source, half = number // PAIR, number % PAIR
-        out[...] = total[
+    parts = [
+        total[
             half * features : (half + 1) * features, source * tokens : (source + 1) * tokens
         ].astype(jnp.bfloat16)
+        for source in range(Z)
+        for half in range(PAIR)
+    ]
+    for out, number in zip(outs[:-1], DIRECT):
+        out[...] = parts[number]
+    for place, number in enumerate(PAIRED):
+        outs[-1][:, place * tokens : (place + 1) * tokens] = parts[number]
 
 
 def combine(slot, high, low, outputs):
     tokens, features = slot.shape[1], outputs[0].shape[2]
     flops = 4 * slot.size * outputs[0].shape[1] * features
-    shape = jax.ShapeDtypeStruct((features // PAIR, tokens // Z), jnp.bfloat16)
-    return whole(
-        combine_kernel, [slot, high, low, *outputs], [shape] * (Z * PAIR), flops, "combine"
-    )
+    sizes = [tokens // Z] * len(DIRECT) + [len(PAIRED) * tokens // Z]
+    shapes = [jax.ShapeDtypeStruct((features // PAIR, size), jnp.bfloat16) for size in sizes]
+    return whole(combine_kernel, [slot, high, low, *outputs], shapes, flops, "combine")
 
 
 def local(tokens, routing, gate_weights, owner, weights, grads, first, second):
@@ -304,14 +312,16 @@
 
     returned = plane_shift(expert_out, -1)
 
-    partial = combine(slot, high, low, returned)
+    *parts, paired = combine(slot, high, low, returned)
+    part = dict(zip(DIRECT, parts))
+    paired = shift(paired, dpair=1)
+    here, across = jnp.split(paired.astype(jnp.float32), len(PAIRED), axis=1)
+    across = (part[4].astype(jnp.float32) + across).astype(jnp.bfloat16)
     moved = [arrived[:, place].reshape(state_shape) for place in range(3)]
-    mixed = sum(
-        shift(part, dz=-(number // PAIR), dpair=number % PAIR).astype(jnp.float32)
-        for number, part in enumerate(partial)
-        if number
-    )
-    mixed = (mixed + after(partial[0], *moved).astype(jnp.float32)).T
+    mixed = here + shift(across, dz=-2).astype(jnp.float32)
+    for number in (2, 3, 6, 7):
+        mixed += shift(part[number], dz=-(number // PAIR), dpair=number % PAIR).astype(jnp.float32)
+    mixed = (mixed + after(part[0], *moved).astype(jnp.float32)).T
     return (mixed.astype(jnp.bfloat16), *moved)
 
 

time: 319 us -> 319 us (level)
  starting transfers between devices: 88.6 us -> 79.7 us
  waiting for transfers between devices: 177 us -> 185 us
    ppermute x28 -> x27, starting transfers between devices: 60.3 us -> 50.9 us  [shift(): return lax.ppermute(array, ('expert', 'cuts'), pairs)]
    ppermute x28 -> x27, waiting for transfers between devices: 177 us -> 185 us  [shift(): return lax.ppermute(array, ('expert', 'cuts'), pairs)]
  transfers between devices with their start and end apart: 30 -> 29, of which waited for: 15 -> 14; matrix products, arithmetic and copies ran while one was open for 7% -> 7% of each run, Pallas kernels for 7% -> 7%
where the time goes in v4:
time: 319 us; the launch traced here: 318 us
  waiting for transfers between devices  185 us (58%)
  starting transfers between devices  79.7 us (25%)
  local copies, waits for them, and re-layouts  21.6 us (7%)
  Pallas kernels  20.9 us (7%)
  other arithmetic  9.18 us (3%)
    ppermute x27, waiting for transfers between devices, shift(): return lax.ppermute(array, ('expert', 'cuts'), pairs)  185 us
    ppermute x27, starting transfers between devices, shift(): return lax.ppermute(array, ('expert', 'cuts'), pairs)  50.9 us
    all_to_all x2, starting transfers between devices, exchange(): lax.all_to_all(array, 'expert', split_axis=0, concat_axis=0, tiled=True)  28.8 us
    pallas_call x4, Pallas kernels, whole(): pl.pallas_call(kernel, in_specs=[vmem] * len(inputs), out_specs=[vmem] *...  11.6 us
    pallas_call x1, Pallas kernels, adamw(): pl.pallas_call(adamw_kernel, grid=(steps,), in_specs=[block] * 4, out_spe...  9.3 us
  transfers between devices with their start and end apart: 29, of which 14 were waited for; matrix products, arithmetic and copies ran while one was open for 7% of the time, Pallas kernels for 7%

profile of v4, /device:TPU:1, one launch (start us, length us, event | category | flops | bytes accessed | tf_op | source)
XLA Modules:
  0.0 318.1 jit_solution(2149398129895490690)
XLA Ops:
  1.6 2.6 collective-permute-start
  6.7 3.8 %collective-permute-start.1 = (bf16[128,960]{1,0:T(8,128)(2,1)S(1)}, bf16[128,960]{1,0:T(8,128)(2,1)S(1)}, u32[]{:S(2)}, u32[]{:S(2)}) collective-permute-start(bf16[128,960]{1,0:T(8,128)(2,1)S(1)} %pad_maximum_fusion.12), channel_id=1, source_target_pairs={{0,16},{1,17},{2,18},{3,19},{4,20},{5,21},{6,22},{7,23},{8,24},{9,... | collective-permute-start | bytes 737288 | tf_op jit(solution)/shard_map/ppermute | solution.py:43
  10.5 4.7 %collective-permute-start.2 = (bf16[128,960]{1,0:T(8,128)(2,1)S(1)}, bf16[128,960]{1,0:T(8,128)(2,1)S(1)}, u32[]{:S(2)}, u32[]{:S(2)}) collective-permute-start(bf16[128,960]{1,0:T(8,128)(2,1)S(1)} %pad_maximum_fusion.12), channel_id=1, source_target_pairs={{0,32},{1,33},{2,34},{3,35},{4,36},{5,37},{6,38},{7,39},{8,40},{9,... | collective-permute-start | bytes 737288 | tf_op jit(solution)/shard_map/ppermute | solution.py:43
  15.2 2.4 collective-permute-start.3
  17.6 9.3 %adamw.1 = bf16[32,3,224,128]{3,2,1,0:T(8,128)(2,1)} custom-call(bf16[32,224,128]{2,1,0:T(8,128)(2,1)} %bitcast.100, bf16[32,224,128]{2,1,0:T(8,128)(2,1)} %bitcast.101, bf16[32,224,128]{2,1,0:T(8,128)(2,1)} %bitcast.102, bf16[32,224,128]{2,1,0:T(8,128)(2,1)} %bitcast.103), custom_call_target="tpu_custom_call" | custom-call | flops 11010048 | bytes 12845056 | tf_op jit(solution)/shard_map/adamw/pallas_call | solution.py:64
  26.9 7.5 %all-to-all-start = ((bf16[32,3,224,128]{3,2,1,0:T(8,128)(2,1)}), bf16[32,3,224,128]{3,2,1,0:T(8,128)(2,1)}, u32[]{:S(2)}, u32[]{:S(2)}) async-start(bf16[32,3,224,128]{3,2,1,0:T(8,128)(2,1)} %adamw.1), calls=%async_computation | async-start | bytes 11010048 | tf_op jit(solution)/shard_map/all_to_all | solution.py:95
  34.6 4.5 %collective-permute-done.3 = bf16[128,960]{1,0:T(8,128)(2,1)S(1)} collective-permute-done((bf16[128,960]{1,0:T(8,128)(2,1)S(1)}, bf16[128,960]{1,0:T(8,128)(2,1)S(1)}, u32[]{:S(2)}, u32[]{:S(2)}) %collective-permute-start.3) | collective-permute-done | bytes 245792 | tf_op jit(solution)/shard_map/ppermute | solution.py:43
  39.8 2.4 dispatch.1
  43.4 2.8 slice.95
  48.0 2.8 collective-permute-start.5
  51.8 2.6 collective-permute-start.9
  55.0 41.4 %collective-permute-done.4.refs_1_ = bf16[2,160,896]{2,1,0:T(8,128)(2,1)S(1)} collective-permute-done((bf16[2,160,896]{2,1,0:T(8,128)(2,1)}, bf16[2,160,896]{2,1,0:T(8,128)(2,1)S(1)}, u32[]{:S(2)}, u32[]{:S(2)}) %collective-permute-start.4) | collective-permute-done | bytes 573472 | tf_op jit(solution)/shard_map/ppermute | solution.py:43
  98.4 16.2 %collective-permute-done.5.refs_2_ = bf16[2,160,896]{2,1,0:T(8,128)(2,1)S(1)} collective-permute-done((bf16[2,160,896]{2,1,0:T(8,128)(2,1)}, bf16[2,160,896]{2,1,0:T(8,128)(2,1)S(1)}, u32[]{:S(2)}, u32[]{:S(2)}) %collective-permute-start.5) | collective-permute-done | bytes 573472 | tf_op jit(solution)/shard_map/ppermute | solution.py:43
  122.1 2.6 collective-permute-start.11
  126.4 12.2 %collective-permute-done.11 = bf16[1280,128]{1,0:T(8,128)(2,1)S(1)} collective-permute-done((bf16[1280,128]{1,0:T(8,128)(2,1)S(1)}, bf16[1280,128]{1,0:T(8,128)(2,1)S(1)}, u32[]{:S(2)}, u32[]{:S(2)}) %collective-permute-start.11) | collective-permute-done | bytes 327712 | tf_op jit(solution)/shard_map/ppermute | solution.py:43
  138.6 4.3 %collective-permute-done.13 = bf16[1280,128]{1,0:T(8,128)(2,1)S(1)} collective-permute-done((bf16[1280,128]{1,0:T(8,128)(2,1)S(1)}, bf16[1280,128]{1,0:T(8,128)(2,1)S(1)}, u32[]{:S(2)}, u32[]{:S(2)}) %collective-permute-start.13) | collective-permute-done | bytes 327712 | tf_op jit(solution)/shard_map/ppermute | solution.py:43
  144.5 6.3 %gather_fusion = bf16[32,3,224,128]{3,2,1,0:T(8,128)(2,1)} fusion(bf16[32,3,224,128]{3,2,1,0:T(8,128)(2,1)} %all-to-all-done, s32[1024]{0:T(1024)S(1)} %pad_clamp_fusion), kind=kCustom, calls=%fused_computation | custom fusion | bytes 11010176 | tf_op jit(solution)/shard_map/jit(_take)/gather | solution.py:309
  150.8 21.3 %all-to-all-start.1 = ((bf16[32,3,224,128]{3,2,1,0:T(8,128)(2,1)}), bf16[32,3,224,128]{3,2,1,0:T(8,128)(2,1)}, u32[]{:S(2)}, u32[]{:S(2)}) async-start(bf16[32,3,224,128]{3,2,1,0:T(8,128)(2,1)} %gather_fusion), calls=%async_computation.1 | async-start | bytes 11010048 | tf_op jit(solution)/shard_map/all_to_all | solution.py:95
  173.5 2.5 collective-permute-start.15
  177.1 5.5 %collective-permute-done.14.refs_1_ = bf16[1280,128]{1,0:T(8,128)(2,1)S(1)} collective-permute-done((bf16[1280,128]{1,0:T(8,128)(2,1)S(1)}, bf16[1280,128]{1,0:T(8,128)(2,1)S(1)}, u32[]{:S(2)}, u32[]{:S(2)}) %collective-permute-start.14) | collective-permute-done | bytes 327712 | tf_op jit(solution)/shard_map/ppermute | solution.py:43
  182.6 8.0 %collective-permute-done.15.refs_2_ = bf16[1280,128]{1,0:T(8,128)(2,1)S(1)} collective-permute-done((bf16[1280,128]{1,0:T(8,128)(2,1)S(1)}, bf16[1280,128]{1,0:T(8,128)(2,1)S(1)}, u32[]{:S(2)}, u32[]{:S(2)}) %collective-permute-start.15) | collective-permute-done | bytes 327712 | tf_op jit(solution)/shard_map/ppermute | solution.py:43
  190.6 2.4 down_project.1
  192.9 2.6 collective-permute-start.17
  196.7 36.5 %collective-permute-done.17.refs_1_ = bf16[2,160,896]{2,1,0:T(8,128)(2,1)S(1)} collective-permute-done((bf16[2,160,896]{2,1,0:T(8,128)(2,1)S(1)}, bf16[2,160,896]{2,1,0:T(8,128)(2,1)S(1)}, u32[]{:S(2)}, u32[]{:S(2)}) %collective-permute-start.17) | collective-permute-done | bytes 573472 | tf_op jit(solution)/shard_map/ppermute | solution.py:43
  234.9 16.9 %collective-permute-done.19.refs_3_ = bf16[2,160,896]{2,1,0:T(8,128)(2,1)S(1)} collective-permute-done((bf16[2,160,896]{2,1,0:T(8,128)(2,1)S(1)}, bf16[2,160,896]{2,1,0:T(8,128)(2,1)S(1)}, u32[]{:S(2)}, u32[]{:S(2)}) %collective-permute-start.19) | collective-permute-done | bytes 573472 | tf_op jit(solution)/shard_map/ppermute | solution.py:43
  253.9 2.7 collective-permute-done.20.refs_4_
  256.7 5.3 %combine.1 = (bf16[448,128]{1,0:T(8,128)(2,1)S(1)}, bf16[448,128]{1,0:T(8,128)(2,1)S(1)}, bf16[448,128]{1,0:T(8,128)(2,1)S(1)}, bf16[448,128]{1,0:T(8,128)(2,1)S...) custom-call(s32[8,512]{1,0:T(8,128)S(1)} %reshape.85.slot, ...), custom_call_target="tpu_custom_call" | custom-call | flops 2348810240 | bytes 4407296 | tf_op jit(solution)/shard_map/combine/pallas_call | solution.py:101
  264.7 7.2 %collective-permute-start.24 = (bf16[448,128]{1,0:T(8,128)(2,1)S(1)}, bf16[448,128]{1,0:T(8,128)(2,1)S(1)}, u32[]{:S(2)}, u32[]{:S(2)}) collective-permute-start(bf16[448,128]{1,0:T(8,128)(2,1)S(1)} %get-tuple-element.38), channel_id=1, source_target_pairs={{0,52},{1,53},{2,54},{3,55},{4,48},{5,49},{6,50},{7,51},{8,60},{9,... | collective-permute-start | bytes 344072 | tf_op jit(solution)/shard_map/ppermute | solution.py:43
  272.9 28.2 %collective-permute-done.21 = bf16[448,256]{1,0:T(8,128)(2,1)S(1)} collective-permute-done((bf16[448,256]{1,0:T(8,128)(2,1)S(1)}, bf16[448,256]{1,0:T(8,128)(2,1)S(1)}, u32[]{:S(2)}, u32[]{:S(2)}) %collective-permute-start.21) | collective-permute-done | bytes 229408 | tf_op jit(solution)/shard_map/ppermute | solution.py:43
  301.1 3.4 %collective-permute-start.22 = (bf16[448,128]{1,0:T(8,128)(2,1)S(1)}, bf16[448,128]{1,0:T(8,128)(2,1)S(1)}, u32[]{:S(2)}, u32[]{:S(2)}) collective-permute-start(bf16[448,128]{1,0:T(8,128)(2,1)S(1)} %fusion.6), channel_id=1, source_target_pairs={{0,32},{1,33},{2,34},{3,35},{4,36},{5,37},{6,38},{7,39},{8,40},{9,... | collective-permute-start | bytes 344072 | tf_op jit(solution)/shard_map/ppermute | solution.py:43
  304.5 5.2 %fusion.32 = (bf16[32,1,224,128]{3,2,1,0:T(8,128)(2,1)}, bf16[32,1,224,128]{3,2,1,0:T(8,128)(2,1)}, bf16[32,1,224,128]{3,2,1,0:T(8,128)(2,1)}) fusion(bf16[32,3,224,128]{3,2,1,0:T(8,128)(2,1)} %all-to-all-done.1), kind=kLoop, calls=%fused_computation.95 | loop fusion | bytes 11010048 | tf_op jit(solution)/shard_map/slice | solution.py:320
  309.7 6.8 %collective-permute-done.22 = bf16[448,128]{1,0:T(8,128)(2,1)S(1)} collective-permute-done((bf16[448,128]{1,0:T(8,128)(2,1)S(1)}, bf16[448,128]{1,0:T(8,128)(2,1)S(1)}, u32[]{:S(2)}, u32[]{:S(2)}) %collective-permute-start.22) | collective-permute-done | bytes 114720 | tf_op jit(solution)/shard_map/ppermute | solution.py:43
  (88 shorter events, 34.2 us)
Async XLA Ops:
  1.6 4.9 %collective-permute-start = (bf16[128,448]{1,0:T(8,128)(2,1)S(1)}, bf16[128,448]{1,0:T(8,128)(2,1)S(1)}, u32[]{:S(2)}, u32[]{:S(2)}) collective-permute-start(bf16[128,448]{1,0:T(8,128)(2,1)S(1)} %copy.56), channel_id=1, source_target_pairs={{0,4},{1,5},{2,6},{3,7},{4,0},{5,1},{6,2},{7,3},{8,12},{9,13},{10,... | collective-permute-start | bytes 344072 | tf_op jit(solution)/shard_map/ppermute | solution.py:43
  6.7 27.9 %collective-permute-start.1 = (bf16[128,960]{1,0:T(8,128)(2,1)S(1)}, bf16[128,960]{1,0:T(8,128)(2,1)S(1)}, u32[]{:S(2)}, u32[]{:S(2)}) collective-permute-start(bf16[128,960]{1,0:T(8,128)(2,1)S(1)} %pad_maximum_fusion.12), channel_id=1, source_target_pairs={{0,16},{1,17},{2,18},{3,19},{4,20},{5,21},{6,22},{7,23},{8,24},{9,... | collective-permute-start | bytes 737288 | tf_op jit(solution)/shard_map/ppermute | solution.py:43
  10.5 24.1 %collective-permute-start.2 = (bf16[128,960]{1,0:T(8,128)(2,1)S(1)}, bf16[128,960]{1,0:T(8,128)(2,1)S(1)}, u32[]{:S(2)}, u32[]{:S(2)}) collective-permute-start(bf16[128,960]{1,0:T(8,128)(2,1)S(1)} %pad_maximum_fusion.12), channel_id=1, source_target_pairs={{0,32},{1,33},{2,34},{3,35},{4,36},{5,37},{6,38},{7,39},{8,40},{9,... | collective-permute-start | bytes 737288 | tf_op jit(solution)/shard_map/ppermute | solution.py:43
  15.2 23.9 %collective-permute-start.3 = (bf16[128,960]{1,0:T(8,128)(2,1)S(1)}, bf16[128,960]{1,0:T(8,128)(2,1)S(1)}, u32[]{:S(2)}, u32[]{:S(2)}) collective-permute-start(bf16[128,960]{1,0:T(8,128)(2,1)S(1)} %pad_maximum_fusion.12), channel_id=1, source_target_pairs={{0,48},{1,49},{2,50},{3,51},{4,52},{5,53},{6,54},{7,55},{8,56},{9,... | collective-permute-start | bytes 737288 | tf_op jit(solution)/shard_map/ppermute | solution.py:43
  26.9 117.6 %all-to-all-start = ((bf16[32,3,224,128]{3,2,1,0:T(8,128)(2,1)}), bf16[32,3,224,128]{3,2,1,0:T(8,128)(2,1)}, u32[]{:S(2)}, u32[]{:S(2)}) async-start(bf16[32,3,224,128]{3,2,1,0:T(8,128)(2,1)} %adamw.1), calls=%async_computation | async-start | bytes 11010048 | tf_op jit(solution)/shard_map/all_to_all | solution.py:95
  42.2 54.2 %collective-permute-start.4 = (bf16[2,160,896]{2,1,0:T(8,128)(2,1)}, bf16[2,160,896]{2,1,0:T(8,128)(2,1)S(1)}, u32[]{:S(2)}, u32[]{:S(2)}) collective-permute-start(bf16[2,160,896]{2,1,0:T(8,128)(2,1)} %get-tuple-element.24), channel_id=1, source_target_pairs={{0,64},{1,65},{2,66},{3,67},{4,68},{5,69},{6,70},{7,71},{8,72},{9,... | collective-permute-start | bytes 1720328 | tf_op jit(solution)/shard_map/ppermute | solution.py:43
  48.0 66.7 %collective-permute-start.5 = (bf16[2,160,896]{2,1,0:T(8,128)(2,1)}, bf16[2,160,896]{2,1,0:T(8,128)(2,1)S(1)}, u32[]{:S(2)}, u32[]{:S(2)}) collective-permute-start(bf16[2,160,896]{2,1,0:T(8,128)(2,1)} %get-tuple-element.25), channel_id=1, source_target_pairs={{0,128},{1,129},{2,130},{3,131},{4,132},{5,133},{6,134},{7,135},{8... | collective-permute-start | bytes 1720328 | tf_op jit(solution)/shard_map/ppermute | solution.py:43
  50.8 63.9 %collective-permute-start.6 = (bf16[2,160,896]{2,1,0:T(8,128)(2,1)S(1)}, bf16[2,160,896]{2,1,0:T(8,128)(2,1)S(1)}, u32[]{:S(2)}, u32[]{:S(2)}) collective-permute-start(bf16[2,160,896]{2,1,0:T(8,128)(2,1)S(1)} %get-tuple-element.26), channel_id=1, source_target_pairs={{0,192},{1,193},{2,194},{3,195},{4,196},{5,197},{6,198},{7,199},{8... | collective-permute-start | bytes 1720328 | tf_op jit(solution)/shard_map/ppermute | solution.py:43
  51.8 64.1 %collective-permute-start.9 = (bf16[2,896,128]{2,1,0:T(8,128)(2,1)S(1)}, bf16[2,896,128]{2,1,0:T(8,128)(2,1)}, u32[]{:S(2)}, u32[]{:S(2)}) collective-permute-start(bf16[2,896,128]{2,1,0:T(8,128)(2,1)S(1)} %pad_maximum_fusion.11), channel_id=1, source_target_pairs={{0,3},{1,0},{2,1},{3,2},{4,7},{5,4},{6,5},{7,6},{8,11},{9,8},{10,9... | collective-permute-start | bytes 1376264 | tf_op jit(solution)/shard_map/ppermute | solution.py:43
  54.4 61.5 %collective-permute-start.8 = (bf16[2,896,128]{2,1,0:T(8,128)(2,1)S(1)}, bf16[2,896,128]{2,1,0:T(8,128)(2,1)}, u32[]{:S(2)}, u32[]{:S(2)}) collective-permute-start(bf16[2,896,128]{2,1,0:T(8,128)(2,1)S(1)} %pad_maximum_fusion.10), channel_id=1, source_target_pairs={{0,2},{1,3},{2,0},{3,1},{4,6},{5,7},{6,4},{7,5},{8,10},{9,11},{10,... | collective-permute-start | bytes 1376264 | tf_op jit(solution)/shard_map/ppermute | solution.py:43
  96.4 19.5 %collective-permute-start.7 = (bf16[2,896,128]{2,1,0:T(8,128)(2,1)S(1)}, bf16[2,896,128]{2,1,0:T(8,128)(2,1)}, u32[]{:S(2)}, u32[]{:S(2)}) collective-permute-start(bf16[2,896,128]{2,1,0:T(8,128)(2,1)S(1)} %pad_maximum_fusion.9), channel_id=1, source_target_pairs={{0,1},{1,2},{2,3},{3,0},{4,5},{5,6},{6,7},{7,4},{8,9},{9,10},{10,1... | collective-permute-start | bytes 1376264 | tf_op jit(solution)/shard_map/ppermute | solution.py:43
  115.9 4.5 %collective-permute-start.10 = (bf16[4,160,896]{2,1,0:T(8,128)(2,1)}, bf16[4,160,896]{2,1,0:T(8,128)(2,1)S(1)}, u32[]{:S(2)}, u32[]{:S(2)}) collective-permute-start(bf16[4,160,896]{2,1,0:T(8,128)(2,1)} %after.3), channel_id=1, source_target_pairs={{0,8},{1,9},{2,10},{3,11},{4,12},{5,13},{6,14},{7,15},{8,0},{9,1},... | collective-permute-start | bytes 3440648 | tf_op jit(solution)/shard_map/ppermute | solution.py:43
  120.4 5.3 %copy-start.2 = (s32[32]{0:T(128)S(1)}, s32[32]{0:T(128)}, u32[]{:S(2)}) copy-start(s32[32]{0:T(128)} %param.11) | copy-start | bytes 388
  122.1 16.6 %collective-permute-start.11 = (bf16[1280,128]{1,0:T(8,128)(2,1)S(1)}, bf16[1280,128]{1,0:T(8,128)(2,1)S(1)}, u32[]{:S(2)}, u32[]{:S(2)}) collective-permute-start(bf16[1280,128]{1,0:T(8,128)(2,1)S(1)} %get-tuple-element.28), channel_id=1, source_target_pairs={{0,3},{1,0},{2,1},{3,2},{4,7},{5,4},{6,5},{7,6},{8,11},{9,8},{10,9... | collective-permute-start | bytes 983048 | tf_op jit(solution)/shard_map/ppermute | solution.py:43
  124.6 14.0 %collective-permute-start.12 = (bf16[1280,128]{1,0:T(8,128)(2,1)S(1)}, bf16[1280,128]{1,0:T(8,128)(2,1)S(1)}, u32[]{:S(2)}, u32[]{:S(2)}) collective-permute-start(bf16[1280,128]{1,0:T(8,128)(2,1)S(1)} %get-tuple-element.29), channel_id=1, source_target_pairs={{0,2},{1,3},{2,0},{3,1},{4,6},{5,7},{6,4},{7,5},{8,10},{9,11},{10,... | collective-permute-start | bytes 983048 | tf_op jit(solution)/shard_map/ppermute | solution.py:43
  125.1 17.7 %collective-permute-start.13 = (bf16[1280,128]{1,0:T(8,128)(2,1)S(1)}, bf16[1280,128]{1,0:T(8,128)(2,1)S(1)}, u32[]{:S(2)}, u32[]{:S(2)}) collective-permute-start(bf16[1280,128]{1,0:T(8,128)(2,1)S(1)} %get-tuple-element.30), channel_id=1, source_target_pairs={{0,1},{1,2},{2,3},{3,0},{4,5},{5,6},{6,7},{7,4},{8,9},{9,10},{10,1... | collective-permute-start | bytes 983048 | tf_op jit(solution)/shard_map/ppermute | solution.py:43
  150.8 21.3 %copy-start = (bf16[1280,128]{1,0:T(8,128)(2,1)S(1)}, bf16[1280,128]{1,0:T(8,128)(2,1)}, u32[]{:S(2)}) copy-start(bf16[1280,128]{1,0:T(8,128)(2,1)} %multiply_convert_fusion.refs_0_) | copy-start | bytes 983044
  150.8 153.6 %all-to-all-start.1 = ((bf16[32,3,224,128]{3,2,1,0:T(8,128)(2,1)}), bf16[32,3,224,128]{3,2,1,0:T(8,128)(2,1)}, u32[]{:S(2)}, u32[]{:S(2)}) async-start(bf16[32,3,224,128]{3,2,1,0:T(8,128)(2,1)} %gather_fusion), calls=%async_computation.1 | async-start | bytes 11010048 | tf_op jit(solution)/shard_map/all_to_all | solution.py:95
  172.2 10.4 %collective-permute-start.14 = (bf16[1280,128]{1,0:T(8,128)(2,1)S(1)}, bf16[1280,128]{1,0:T(8,128)(2,1)S(1)}, u32[]{:S(2)}, u32[]{:S(2)}) collective-permute-start(bf16[1280,128]{1,0:T(8,128)(2,1)S(1)} %copy-done), channel_id=1, source_target_pairs={{0,1},{1,2},{2,3},{3,0},{4,5},{5,6},{6,7},{7,4},{8,9},{9,10},{10,1... | collective-permute-start | bytes 983048 | tf_op jit(solution)/shard_map/ppermute | solution.py:43
  173.5 17.1 %collective-permute-start.15 = (bf16[1280,128]{1,0:T(8,128)(2,1)S(1)}, bf16[1280,128]{1,0:T(8,128)(2,1)S(1)}, u32[]{:S(2)}, u32[]{:S(2)}) collective-permute-start(bf16[1280,128]{1,0:T(8,128)(2,1)S(1)} %copy-done), channel_id=1, source_target_pairs={{0,2},{1,3},{2,0},{3,1},{4,6},{5,7},{6,4},{7,5},{8,10},{9,11},{10,... | collective-permute-start | bytes 983048 | tf_op jit(solution)/shard_map/ppermute | solution.py:43
  175.9 14.7 %collective-permute-start.16 = (bf16[1280,128]{1,0:T(8,128)(2,1)S(1)}, bf16[1280,128]{1,0:T(8,128)(2,1)S(1)}, u32[]{:S(2)}, u32[]{:S(2)}) collective-permute-start(bf16[1280,128]{1,0:T(8,128)(2,1)S(1)} %copy-done), channel_id=1, source_target_pairs={{0,3},{1,0},{2,1},{3,2},{4,7},{5,4},{6,5},{7,6},{8,11},{9,8},{10,9... | collective-permute-start | bytes 983048 | tf_op jit(solution)/shard_map/ppermute | solution.py:43
  192.9 40.3 %collective-permute-start.17 = (bf16[2,160,896]{2,1,0:T(8,128)(2,1)S(1)}, bf16[2,160,896]{2,1,0:T(8,128)(2,1)S(1)}, u32[]{:S(2)}, u32[]{:S(2)}) collective-permute-start(bf16[2,160,896]{2,1,0:T(8,128)(2,1)S(1)} %get-tuple-element.32), channel_id=1, source_target_pairs={{0,192},{1,193},{2,194},{3,195},{4,196},{5,197},{6,198},{7,199},{8... | collective-permute-start | bytes 1720328 | tf_op jit(solution)/shard_map/ppermute | solution.py:43
  195.6 39.3 %collective-permute-start.18 = (bf16[2,160,896]{2,1,0:T(8,128)(2,1)S(1)}, bf16[2,160,896]{2,1,0:T(8,128)(2,1)S(1)}, u32[]{:S(2)}, u32[]{:S(2)}) collective-permute-start(bf16[2,160,896]{2,1,0:T(8,128)(2,1)S(1)} %get-tuple-element.33), channel_id=1, source_target_pairs={{0,128},{1,129},{2,130},{3,131},{4,132},{5,133},{6,134},{7,135},{8... | collective-permute-start | bytes 1720328 | tf_op jit(solution)/shard_map/ppermute | solution.py:43
  196.1 55.7 %collective-permute-start.19 = (bf16[2,160,896]{2,1,0:T(8,128)(2,1)S(1)}, bf16[2,160,896]{2,1,0:T(8,128)(2,1)S(1)}, u32[]{:S(2)}, u32[]{:S(2)}) collective-permute-start(bf16[2,160,896]{2,1,0:T(8,128)(2,1)S(1)} %get-tuple-element.34), channel_id=1, source_target_pairs={{0,64},{1,65},{2,66},{3,67},{4,68},{5,69},{6,70},{7,71},{8,72},{9,... | collective-permute-start | bytes 1720328 | tf_op jit(solution)/shard_map/ppermute | solution.py:43
  253.0 3.6 %collective-permute-start.20 = (bf16[4,160,896]{2,1,0:T(8,128)(2,1)}, bf16[4,160,896]{2,1,0:T(8,128)(2,1)}, u32[]{:S(2)}, u32[]{:S(2)}) collective-permute-start(bf16[4,160,896]{2,1,0:T(8,128)(2,1)} %pad_maximum_fusion.1), channel_id=1, source_target_pairs={{0,8},{1,9},{2,10},{3,11},{4,12},{5,13},{6,14},{7,15},{8,0},{9,1},... | collective-permute-start | bytes 3440648 | tf_op jit(solution)/shard_map/ppermute | solution.py:43
  261.9 0.6 copy-start.1
  262.6 38.5 %collective-permute-start.21 = (bf16[448,256]{1,0:T(8,128)(2,1)S(1)}, bf16[448,256]{1,0:T(8,128)(2,1)S(1)}, u32[]{:S(2)}, u32[]{:S(2)}) collective-permute-start(bf16[448,256]{1,0:T(8,128)(2,1)S(1)} %get-tuple-element.35), channel_id=1, source_target_pairs={{0,4},{1,5},{2,6},{3,7},{4,0},{5,1},{6,2},{7,3},{8,12},{9,13},{10,... | collective-permute-start | bytes 688136 | tf_op jit(solution)/shard_map/ppermute | solution.py:43
  262.6 47.0 %collective-permute-start.23 = (bf16[448,128]{1,0:T(8,128)(2,1)S(1)}, bf16[448,128]{1,0:T(8,128)(2,1)S(1)}, u32[]{:S(2)}, u32[]{:S(2)}) collective-permute-start(bf16[448,128]{1,0:T(8,128)(2,1)S(1)} %get-tuple-element.37), channel_id=1, source_target_pairs={{0,48},{1,49},{2,50},{3,51},{4,52},{5,53},{6,54},{7,55},{8,56},{9,... | collective-permute-start | bytes 344072 | tf_op jit(solution)/shard_map/ppermute | solution.py:43
  264.7 44.9 %collective-permute-start.24 = (bf16[448,128]{1,0:T(8,128)(2,1)S(1)}, bf16[448,128]{1,0:T(8,128)(2,1)S(1)}, u32[]{:S(2)}, u32[]{:S(2)}) collective-permute-start(bf16[448,128]{1,0:T(8,128)(2,1)S(1)} %get-tuple-element.38), channel_id=1, source_target_pairs={{0,52},{1,53},{2,54},{3,55},{4,48},{5,49},{6,50},{7,51},{8,60},{9,... | collective-permute-start | bytes 344072 | tf_op jit(solution)/shard_map/ppermute | solution.py:43
  272.0 37.7 %collective-permute-start.25 = (bf16[448,128]{1,0:T(8,128)(2,1)S(1)}, bf16[448,128]{1,0:T(8,128)(2,1)S(1)}, u32[]{:S(2)}, u32[]{:S(2)}) collective-permute-start(bf16[448,128]{1,0:T(8,128)(2,1)S(1)} %get-tuple-element.39), channel_id=1, source_target_pairs={{0,16},{1,17},{2,18},{3,19},{4,20},{5,21},{6,22},{7,23},{8,24},{9,... | collective-permute-start | bytes 344072 | tf_op jit(solution)/shard_map/ppermute | solution.py:43
  272.0 37.7 %collective-permute-start.26 = (bf16[448,128]{1,0:T(8,128)(2,1)S(1)}, bf16[448,128]{1,0:T(8,128)(2,1)S(1)}, u32[]{:S(2)}, u32[]{:S(2)}) collective-permute-start(bf16[448,128]{1,0:T(8,128)(2,1)S(1)} %get-tuple-element.40), channel_id=1, source_target_pairs={{0,20},{1,21},{2,22},{3,23},{4,16},{5,17},{6,18},{7,19},{8,28},{9,... | collective-permute-start | bytes 344072 | tf_op jit(solution)/shard_map/ppermute | solution.py:43
  301.1 15.3 %collective-permute-start.22 = (bf16[448,128]{1,0:T(8,128)(2,1)S(1)}, bf16[448,128]{1,0:T(8,128)(2,1)S(1)}, u32[]{:S(2)}, u32[]{:S(2)}) collective-permute-start(bf16[448,128]{1,0:T(8,128)(2,1)S(1)} %fusion.6), channel_id=1, source_target_pairs={{0,32},{1,33},{2,34},{3,35},{4,36},{5,37},{6,38},{7,39},{8,40},{9,... | collective-permute-start | bytes 344072 | tf_op jit(solution)/shard_map/ppermute | solution.py:43
